TPU v7x, 32 devices: a whole 2x2x4 slice. The times are simulated.
32 devices in a mesh: fsdp: 8 (over y, x, core), seq: 4 (over z).
Axes of the slice: x: 2, y: 2, z: 4, core: 2. Of those that a mesh axis runs over, the one named last changes fastest.
Arguments:
- tokens: bfloat16 [24, 1024, 768], P('fsdp', 'seq'), may hold values from -6 to 6
- lengths: int32 [24, 10], P('fsdp'), may hold values from 0 to 1024, as said below
- pictures: int32 [24, 1024], P('fsdp', 'seq'), may hold values from 0 to 8, as said below
- first_gain: bfloat16 [768], P('fsdp'), may hold values from 0.5 to 1.5
- mix_weight: bfloat16 [768, 2304], P('fsdp'), may hold values from -0.21875 to 0.21875
- query_gain: bfloat16 [768], P('fsdp'), may hold values from 0.796875 to 2
- key_gain: bfloat16 [768], P('fsdp'), may hold values from 0.796875 to 2
- out_weight: bfloat16 [768, 768], P('fsdp'), may hold values from -1.75 to 1.75
- second_gain: bfloat16 [768], P('fsdp'), may hold values from 0.5 to 1.5
- up_weight: bfloat16 [768, 3072], P('fsdp'), may hold values from -0.21875 to 0.21875
- down_weight: bfloat16 [3072, 768], P('fsdp'), may hold values from -0.109375 to 0.109375
- cotangent: bfloat16 [24, 1024, 768], P('fsdp', 'seq'), may hold values from -6 to 6
Outputs:
- output: bfloat16 [24, 1024, 768], P('fsdp', 'seq')
- input_grad: bfloat16 [24, 1024, 768], P('fsdp', 'seq')
- first_gain_grad: float32 [768], P('fsdp')
- mix_weight_grad: float32 [768, 2304], P('fsdp')
- query_gain_grad: float32 [768], P('fsdp')
- key_gain_grad: float32 [768], P('fsdp')
- out_weight_grad: float32 [768, 768], P('fsdp')
- second_gain_grad: float32 [768], P('fsdp')
- up_weight_grad: float32 [768, 3072], P('fsdp')
- down_weight_grad: float32 [3072, 768], P('fsdp')
Inputs may be any that keep to these rules, and one draw needn't show every extreme that they name: In each row the nonzero lengths come first, each 100 or more, and sum to 922 or more and 1024 or less; later entries are 0. Rows whose index is a multiple of 8 hold one picture of 1024 patches; rows whose index leaves 1 after division by 8 hold (922) // 100 pictures. Slot s of a row holds the number (from 0, in the order of lengths) of the picture whose patches cover s when the row's pictures are laid end to end by lengths; slots after the last picture hold the last picture's number. Numbers never fall along a row.
All inputs are finite; a program needn't handle non-finite values.
Results may differ from a plain program's by a relative error of at most 0.017.
Values may be sent and summed in bfloat16 or wider, within the bound.
A program may use at most 128 MiB of HBM per device.

v0:
```python
import functools

import jax
import jax.numpy as jnp
from jax import lax
from jax.experimental import pallas as pl
from jax.experimental.pallas import tpu as pltpu
from jax.sharding import Mesh, PartitionSpec as P

HEADS = 12
HEAD = 64
EPSILON = 1e-06
BLOCK = 256
STEP = 512
MARK = 32.0
EXP2_FACTOR = HEAD**-0.5 * 1.4426950408889634
F32 = jnp.float32
BF16 = jnp.bfloat16
VMEM_LIMIT = 56 * 1024 * 1024

SEQ = ("zp", "zq")
COLUMN = ("core", "zp", "zq")
KEEP = [
    (core * 4 + z, (z // 2) * 4 + 2 * core + z % 2) for core in range(2) for z in range(4)
]
CROSS = [
    (core * 4 + z, (z // 2) * 4 + 2 * core + 1 - z % 2) for core in range(2) for z in range(4)
]


def swap(array, name, bit=1):
    count = lax.axis_size(name)
    return lax.ppermute(array, name, [(i, i ^ bit) for i in range(count)])


def pick(array, index, axis=0):
    return lax.dynamic_index_in_dim(array, index, axis, keepdims=False)


def group_ones(scale):
    row = lax.broadcasted_iota(jnp.int32, (128, 128), 0) // HEAD
    column = lax.broadcasted_iota(jnp.int32, (128, 128), 1) // HEAD
    return jnp.where(row == column, scale, 0.0).astype(BF16)


def group_sum(values, ones):
    return jnp.dot(values.astype(BF16), ones, preferred_element_type=F32)


def group_sum_fine(values, ones):
    high = values.astype(BF16)
    return group_sum(high, ones) + group_sum(values - high.astype(F32), ones)


def project_kernel(x_ref, gain_ref, weight_ref, qg_ref, kg_ref, normed_ref, q_ref, k_ref, v_ref, raw_ref):
    width = q_ref.shape[1]
    x = x_ref[...].astype(F32)
    center = x - jnp.mean(x, axis=-1, keepdims=True)
    spread = jnp.mean(center * center, axis=-1, keepdims=True)
    normed = (center * lax.rsqrt(spread + EPSILON) * gain_ref[...]).astype(BF16)
    normed_ref[...] = normed
    mixed = jnp.dot(normed, weight_ref[...], preferred_element_type=F32)
    raw_ref[...] = mixed[:, : 2 * width].astype(BF16)
    ones = group_ones(1.0 / HEAD)
    for part, (out_ref, g_ref) in enumerate(((q_ref, qg_ref), (k_ref, kg_ref))):
        for at in range(0, width, 128):
            raw = mixed[:, part * width + at : part * width + at + 128]
            c = raw - group_sum_fine(raw, ones)
            n = c * lax.rsqrt(group_sum(c * c, ones) + EPSILON)
            out_ref[:, at : at + 128] = (n * g_ref[:, at : at + 128]).astype(BF16)
    v_ref[...] = mixed[:, 2 * width :].astype(BF16)


def nt(a, b):
    return lax.dot_general(a, b, (((1,), (1,)), ((), ())), preferred_element_type=F32)


def tn(a, b):
    return lax.dot_general(a, b, (((0,), (0,)), ((), ())), preferred_element_type=F32)


def slots(queries, length, part):
    at = lax.broadcasted_iota(jnp.int32, (queries, 128), 0)
    if queries == length:
        return at
    return at % part + part * (lax.axis_index("zq") + 2 * (at // part))


def own_rows(ref, start, count, queries, part):
    if queries == ref.shape[0]:
        return ref[pl.ds(start, count), :]
    zq = lax.axis_index("zq")
    pieces = [
        ref[pl.ds(pl.multiple_of((zq + 2 * i) * part, part), part), :]
        for i in range(start // part, (start + count) // part)
    ]
    return jnp.concatenate(pieces, axis=0)


def query_marks(bounds_ref, place, queries, length, part, pics):
    at = slots(queries, length, part)
    inside = (at >= bounds_ref[0:1, :]) & (at < bounds_ref[2:3, :])
    values = jnp.where(inside, MARK, 0.0)
    return jnp.where(place == pics, MARK, values).astype(BF16)


def key_marks(bounds_ref, place, length, pics):
    at = lax.broadcasted_iota(jnp.int32, (length, 128), 0)
    inside = (at >= bounds_ref[0:1, :]) & (at < bounds_ref[1:2, :])
    values = jnp.where(inside, MARK, 0.0)
    values = jnp.where(place == pics, -MARK, values)
    return jnp.where((place > pics) & (place < pics + 4), 1.0, values).astype(BF16)


def attend_kernel(pics, q_ref, k_ref, v_ref, bounds_ref, out_ref, aug_ref, kaug, vaug, qaug):
    length = k_ref.shape[0]
    queries = out_ref.shape[0]
    part = length // 4
    lane = lax.broadcasted_iota(jnp.int32, (1, 128), 1)
    place = lane % HEAD
    sides = [lane < HEAD, lane >= HEAD]
    kmarks = key_marks(bounds_ref, place, length, pics)
    qmarks = query_marks(bounds_ref, place, queries, length, part, pics)
    qaug[...] = qmarks
    for h in range(2):
        kaug[h] = jnp.where(sides[h], k_ref[...], kmarks)
        vaug[h] = jnp.where(sides[h], v_ref[...], jnp.ones_like(v_ref))
    for b in range(queries // STEP):
        rows = pl.ds(b * STEP, STEP)
        mine = own_rows(q_ref, b * STEP, STEP, queries, part)
        query = [jnp.where(sides[h], mine, qaug[rows, :]) for h in range(2)]
        total = [jnp.zeros((STEP, 128), F32)] * 2
        for j in range(length // STEP):
            keys = pl.ds(j * STEP, STEP)
            scores = [nt(query[h], kaug[h, keys, :]) for h in range(2)]
            weights = [jnp.exp2(x * EXP2_FACTOR).astype(BF16) for x in scores]
            total = [
                total[h] + jnp.dot(weights[h], vaug[h, keys, :], preferred_element_type=F32) for h in range(2)
            ]
        results = []
        for h in range(2):
            results.append(total[h] / pltpu.roll(total[h], HEAD, 1))
            log_total = jnp.log(jnp.where(sides[h], 1.0, total[h])) * -(HEAD**0.5)
            first = log_total.astype(BF16)
            rest = log_total - first.astype(F32)
            middle = rest.astype(BF16)
            last = (rest - middle.astype(F32)).astype(BF16)
            logs = jnp.where(place == pics + 1, first, jnp.where(place == pics + 2, middle, last))
            slot = jnp.logical_not(sides[h]) & (place > pics) & (place < pics + 4)
            aug_ref[h, rows, :] = jnp.where(slot, logs, query[h])
        out_ref[rows, :] = jnp.where(sides[0], results[0], results[1]).astype(BF16)


def head_norm_back(e, raw, gain, means):
    raw = raw.astype(F32)
    c = raw - group_sum(raw, means)
    r = lax.rsqrt(group_sum(c * c, means) + EPSILON)
    n = c * r
    t = e * gain
    grad = r * (t - group_sum(t, means) - n * group_sum(t * n, means))
    return grad.astype(BF16), jnp.sum(e * n, axis=0, keepdims=True)


def attend_back_kernel(
    pics, aug_ref, k_ref, v_ref, out_ref, do_ref, rawq_ref, rawk_ref, qg_ref, kg_ref, bounds_ref,
    dq_ref, dk_ref, dv_ref, qgg_ref, kgg_ref, kaug, vaug, doaug, qsum, ksum,
):
    length = k_ref.shape[0]
    queries = do_ref.shape[0]
    part = length // 4
    whole = queries == length
    lane = lax.broadcasted_iota(jnp.int32, (1, 128), 1)
    place = lane % HEAD
    sides = [lane < HEAD, lane >= HEAD]
    kmarks = key_marks(bounds_ref, place, length, pics)
    vmarks = jnp.where(place < 2, 1.0, 0.0).astype(BF16)
    ones = group_ones(1.0)
    inner = group_sum_fine(do_ref[...].astype(F32) * out_ref[...].astype(F32), ones)
    inner = -pltpu.roll(inner, HEAD, 1)
    inner_high = inner.astype(BF16)
    inner_low = (inner - inner_high.astype(F32)).astype(BF16)
    zero = jnp.zeros((), BF16)
    gmarks = jnp.where(place == 0, inner_high, jnp.where(place == 1, inner_low, zero))
    for h in range(2):
        kaug[h] = jnp.where(sides[h], k_ref[...], kmarks)
        vaug[h] = jnp.where(sides[h], v_ref[...], vmarks)
        doaug[h] = jnp.where(sides[h], do_ref[...], gmarks)
    for b in range(length // STEP):
        keys = pl.ds(b * STEP, STEP)
        key = [kaug[h, keys, :] for h in range(2)]
        value = [vaug[h, keys, :] for h in range(2)]
        dk = [jnp.zeros((STEP, 128), F32)] * 2
        dv = [jnp.zeros((STEP, 128), F32)] * 2
        for j in range(queries // STEP):
            rows = pl.ds(j * STEP, STEP)
            query = [aug_ref[h, rows, :] for h in range(2)]
            grad = [doaug[h, rows, :] for h in range(2)]
            scores = [nt(key[h], query[h]) for h in range(2)]
            soft_grad = [nt(value[h], grad[h]) for h in range(2)]
            weights = [jnp.exp2(x * EXP2_FACTOR) for x in scores]
            score_grad = [(weights[h] * soft_grad[h]).astype(BF16) for h in range(2)]
            for h in range(2):
                part_sum = tn(score_grad[h], key[h])
                if b == 0:
                    qsum[h, rows, :] = part_sum
                else:
                    qsum[h, rows, :] += part_sum
                dk[h] = dk[h] + jnp.dot(score_grad[h], query[h], preferred_element_type=F32)
                dv[h] = dv[h] + jnp.dot(weights[h].astype(BF16), grad[h], preferred_element_type=F32)
        ksum[keys, :] = jnp.where(sides[0], dk[0], dk[1]) * HEAD**-0.5
        dv_ref[keys, :] = jnp.where(sides[0], dv[0], dv[1]).astype(BF16)

    means = group_ones(1.0 / HEAD)
    gain_sum = jnp.zeros((1, 128), F32)
    for b in range(queries // part):
        rows = pl.ds(b * part, part)
        e = jnp.where(sides[0], qsum[0, rows, :], qsum[1, rows, :]) * HEAD**-0.5
        raw = own_rows(rawq_ref, b * part, part, queries, part)
        dq_ref[rows, :], more = head_norm_back(e.astype(BF16).astype(F32), raw, qg_ref[...], means)
        gain_sum = gain_sum + more
    qgg_ref[...] = gain_sum
    gain_sum = jnp.zeros((1, 128), F32)
    for b in range(length // part):
        rows = pl.ds(b * part, part)
        e = ksum[rows, :].astype(BF16)
        if whole:
            dk_ref[rows, :], more = head_norm_back(e.astype(F32), rawk_ref[rows, :], kg_ref[...], means)
            gain_sum = gain_sum + more
        else:
            dk_ref[rows, :] = e
    kgg_ref[...] = gain_sum


def attend_back(aug, k, v, out, do, raw, query_gain, key_gain, bounds, pics):
    length, width = k.shape
    queries = do.shape[0]
    pairs = width // 128
    column = pl.BlockSpec((length, 128), lambda p: (0, p))
    own = pl.BlockSpec((queries, 128), lambda p: (0, p))
    gain = pl.BlockSpec((1, 128), lambda p: (0, p))
    return pl.pallas_call(
        functools.partial(attend_back_kernel, pics),
        grid=(pairs,),
        in_specs=[
            pl.BlockSpec((2, queries, 128), lambda p: (p, 0, 0)),
            column,
            column,
            own,
            own,
            column,
            pl.BlockSpec((length, 128), lambda p: (0, pairs + p)),
            gain,
            gain,
            pl.BlockSpec((8, 128), lambda p: (0, 0)),
        ],
        out_specs=[own, column, column, gain, gain],
        scratch_shapes=[
            pltpu.VMEM((2, length, 128), BF16),
            pltpu.VMEM((2, length, 128), BF16),
            pltpu.VMEM((2, queries, 128), BF16),
            pltpu.VMEM((2, queries, 128), F32),
            pltpu.VMEM((length, 128), F32),
        ],
        out_shape=[
            jax.ShapeDtypeStruct((queries, width), BF16),
            jax.ShapeDtypeStruct((length, width), BF16),
            jax.ShapeDtypeStruct((length, width), BF16),
            jax.ShapeDtypeStruct((1, width), F32),
            jax.ShapeDtypeStruct((1, width), F32),
        ],
        compiler_params=pltpu.CompilerParams(vmem_limit_bytes=VMEM_LIMIT),
        cost_estimate=pl.CostEstimate(
            flops=40 * length * queries * width, bytes_accessed=length * width * 20, transcendentals=0
        ),
        name="attend_back",
    )(aug, k, v, out, do, raw, raw, query_gain, key_gain, bounds)


def shared_keys_kernel(dk_ref, dv_ref, gotk_ref, gotv_ref, rawk_ref, kg_ref, outk_ref, outv_ref, kgg_ref):
    count = outk_ref.shape[0]
    part = count // 2
    means = group_ones(1.0 / HEAD)
    gain_sum = jnp.zeros((1, 128), F32)
    for b in range(2):
        rows = pl.ds(b * part, part)
        own = lambda ref: own_rows(ref, b * part, part, count, part)
        e = own(dk_ref).astype(F32) + gotk_ref[rows, :].astype(F32)
        outk_ref[rows, :], more = head_norm_back(e, own(rawk_ref), kg_ref[...], means)
        gain_sum = gain_sum + more
        outv_ref[rows, :] = (own(dv_ref).astype(F32) + gotv_ref[rows, :].astype(F32)).astype(BF16)
    kgg_ref[...] = gain_sum


def shared_keys(dk, dv, got_k, got_v, raw, key_gain):
    length, width = dk.shape
    pairs = width // 128
    column = pl.BlockSpec((length, 128), lambda p: (0, p))
    own = pl.BlockSpec((length // 2, 128), lambda p: (0, p))
    gain = pl.BlockSpec((1, 128), lambda p: (0, p))
    return pl.pallas_call(
        shared_keys_kernel,
        grid=(pairs,),
        in_specs=[column, column, own, own, pl.BlockSpec((length, 128), lambda p: (0, pairs + p)), gain],
        out_specs=[own, own, gain],
        out_shape=[
            jax.ShapeDtypeStruct((length // 2, width), BF16),
            jax.ShapeDtypeStruct((length // 2, width), BF16),
            jax.ShapeDtypeStruct((1, width), F32),
        ],
        compiler_params=pltpu.CompilerParams(vmem_limit_bytes=VMEM_LIMIT),
        name="shared_keys",
    )(dk, dv, got_k, got_v, raw, key_gain)


def gelu_pair(h):
    size = jnp.abs(h)
    bell = jnp.exp2(h * h * -0.7213475204444817)
    t = 1.0 / (1.0 + 0.23164189 * size)
    series = t * (0.127414796 + t * (-0.142248368 + t * (0.7107068705 + t * (-0.7265760135 + t * 0.5307027145))))
    tail = series * bell
    below = jnp.where(h < 0.0, tail, 1.0 - tail)
    return h * below, below + h * (bell * 0.3989422804014327)


def norm_parts(values):
    center = values - jnp.mean(values, axis=-1, keepdims=True)
    spread = lax.rsqrt(jnp.mean(center * center, axis=-1, keepdims=True) + EPSILON)
    return center * spread, spread


def norm_back(upstream, n, r, gain):
    t = upstream * gain
    grad = r * (t - jnp.mean(t, axis=-1, keepdims=True) - n * jnp.mean(t * n, axis=-1, keepdims=True))
    return grad, jnp.sum(upstream * n, axis=0, keepdims=True)


MESH_ID = pl.DeviceIdType.MESH


def here():
    return lax.axis_index("chip"), lax.axis_index("core"), lax.axis_index("zp"), lax.axis_index("zq")


def remote(source, target, sems, at, device):
    sent, got = sems
    return pltpu.make_async_remote_copy(
        src_ref=source, dst_ref=target, send_sem=sent.at[at], recv_sem=got.at[at],
        device_id=device, device_id_type=MESH_ID,
    )


def greet(devices, maybe=None, moves=None):
    barrier = pltpu.get_barrier_semaphore()
    for device in devices:
        pl.semaphore_signal(barrier, inc=1, device_id=device, device_id_type=MESH_ID)
    if maybe is None:
        pl.semaphore_wait(barrier, len(devices))
        return

    @pl.when(moves)
    def _():
        pl.semaphore_signal(barrier, inc=1, device_id=maybe, device_id_type=MESH_ID)

    pl.semaphore_wait(barrier, len(devices) + jnp.where(moves, 1, 0))


def rows_at(start, count):
    return pl.ds(pl.multiple_of(start, 16), count)


def write_bounds(pics, lens_ref, bounds_ref, zp, zq, length):
    lane = lax.broadcasted_iota(jnp.int32, (8, 128), 1)
    lens = jnp.where(zp == 0, lens_ref[0], lens_ref[1])
    ends = lens
    for hop in (1, 2, 4, 8):
        ends = ends + jnp.where(lane >= hop, pltpu.roll(ends, hop, 1), 0)
    starts = ends - lens
    last = (lens > 0) & (pltpu.roll(lens, 127, 1) == 0)
    query_ends = jnp.where(last, length, ends)
    total = jnp.max(jnp.where(lane < pics, ends, 0), axis=1, keepdims=True)

    def both(values):
        values = jnp.where(lane < HEAD, jnp.where(lane < pics, values, 2 * length), 0)
        return values + pltpu.roll(values, HEAD, 1)

    tables = [both(starts), both(ends), both(query_ends), jnp.broadcast_to(total, (8, 128))]
    for t in range(4):
        table = tables[t]
        bounds_ref[0, t : t + 1, :] = jnp.where(zq == 0, table[0:1], table[1:2])
        bounds_ref[1, t : t + 1, :] = table[2:3]
    bounds_ref[:, 4:, :] = jnp.zeros((2, 4, 128), jnp.int32)


def forward_kernel(square, pics, *refs):
    refs = list(refs)
    take = lambda count: [refs.pop(0) for _ in range(count)]
    tokens_ref, cot_ref, lens_ref, mix_ref, gains_ref = take(5)
    if square:
        up_ref, down_ref, outw_ref = take(3)
    else:
        gain_first, gain_query, gain_key = take(3)
    x_out, bounds_ref, mix_hbm, second_ref, query_out, key_out, cot_hbm = take(7)
    names = ("normed", "k", "v", "raw", "out", "aug")
    outs = [dict(zip(names, take(6))) for _ in range(2)]
    if square:
        up_hbm, down_hbm, outw_hbm = take(3)
    row_ref, shared_ref, cot_out, lens_out = take(4)
    scratch = [dict(zip(names + ("q",), take(7))) for _ in range(2)]
    kaug, vaug, qaug = take(3)
    if square:
        mix_out, gains_out, gain_first, gain_query, gain_key, up_out, down_out, outw_out = take(8)
    sent, got, local_sem, write_sem = take(4)

    chip, core, zp, zq = here()
    z = 2 * zp + zq
    part = tokens_ref.shape[1]
    half, length = 2 * part, 4 * part
    sems = (sent, got)
    partner = (chip, 1 - core, zp, zq)
    side = (chip, core, zp, 1 - zq)
    keep = (chip, zp, core, zq)
    cross = (chip, zp, core, 1 - zq)
    moves = core != zp
    near_x = (chip ^ 1, core, zp, zq)
    near_y = (chip ^ 2, core, zp, zq)
    greet([partner, side, cross] + ([near_x, near_y] if square else []), keep, moves)

    def quarter(ref, index):
        return ref.at[rows_at(index * part, part)]

    own_row = remote(tokens_ref.at[zq], quarter(row_ref, z), sems, 0, keep)
    own_shared = remote(tokens_ref.at[2], quarter(shared_ref, z), sems, 2, keep)
    stay_row = pltpu.make_async_copy(tokens_ref.at[zq], quarter(row_ref, z), local_sem.at[0])
    stay_shared = pltpu.make_async_copy(tokens_ref.at[2], quarter(shared_ref, z), local_sem.at[1])

    @pl.when(moves)
    def _():
        own_row.start()

    @pl.when(jnp.logical_not(moves))
    def _():
        stay_row.start()

    cross_row = remote(tokens_ref.at[1 - zq], quarter(row_ref, z), sems, 1, cross)
    cross_row.start()

    @pl.when(moves)
    def _():
        own_shared.start()

    @pl.when(jnp.logical_not(moves))
    def _():
        stay_shared.start()

    lens_copy = remote(lens_ref, lens_out.at[core], sems, 8, partner)
    lens_copy.start()
    lens_stay = pltpu.make_async_copy(lens_ref, lens_out.at[core], local_sem.at[2])
    lens_stay.start()
    waits = []
    if square:
        shard = mix_ref.shape[1]
        down_rows = down_ref.shape[0]
        mine, theirs = 2 * chip + core, 2 * chip + 1 - core
        slot = [9]

        def send(source, target, device):
            copy = remote(source, target, sems, slot[0], device)
            slot[0] += 1
            copy.start()
            waits.append(copy)
            return copy

        def stay(source, target, at):
            copy = pltpu.make_async_copy(source, target, local_sem.at[at])
            copy.start()
            return copy

        def block(ref, start, count):
            return ref.at[rows_at(start, count)]

        mix_piece = lambda index: (block(mix_out, index * shard, shard), gains_out.at[index])

        def send_mix(sources, index, device):
            return [send(source, target, device) for source, target in zip(sources, mix_piece(index))]

        def arrived(copies):
            for copy in copies:
                copy.wait_recv()

        x_mine, y_other = 2 * (chip ^ 1) + core, 2 * (chip ^ 2) + 1 - core
        to_core = send_mix((mix_ref.at[1 - core], gains_ref), mine, partner)
        a_x = send_mix((mix_ref.at[core], gains_ref), mine, near_x)
        a_y = send_mix((mix_ref.at[core], gains_ref), mine, near_y)
        up_core = send(up_ref.at[1 - core], block(up_out, mine * shard, shard), partner)
        out_core = send(outw_ref, block(outw_out, mine * shard, shard), partner)
        stays = [
            stay(mix_ref.at[core], mix_piece(mine)[0], 3),
            stay(gains_ref, gains_out.at[mine], 4),
            stay(up_ref.at[core], block(up_out, mine * shard, shard), 5),
            stay(down_ref, block(down_out, chip * down_rows, down_rows), 6),
            stay(outw_ref, block(outw_out, mine * shard, shard), 7),
        ]
        arrived(to_core)
        b_x = send_mix(mix_piece(theirs), theirs, near_x)
        b_y = send_mix(mix_piece(theirs), theirs, near_y)
        arrived(a_x)
        a_far = send_mix(mix_piece(x_mine), x_mine, near_y)
        arrived(b_y)
        b_far = send_mix(mix_piece(y_other), y_other, near_x)
        for copy in stays:
            copy.wait()
        arrived([up_core])
        dhalf, ohalf = down_rows // 2, shard // 2

        def bundle(first, from_chip):
            same, twin = 2 * from_chip + core, 2 * from_chip + 1 - core
            part_of = 0 if first else 1
            return [
                block(up_out, (same if first else twin) * shard, shard),
                block(down_out, from_chip * down_rows + part_of * dhalf, dhalf),
                block(outw_out, same * shard + part_of * ohalf, ohalf),
            ]

        def send_bundle(first, from_chip, device):
            return [send(ref, ref, device) for ref in bundle(first, from_chip)]

        first_x = send_bundle(True, chip, near_x)
        first_y = send_bundle(True, chip, near_y)
        second_x = send_bundle(False, chip, near_x)
        second_y = send_bundle(False, chip, near_y)

    lens_copy.wait()
    lens_stay.wait()
    write_bounds(pics, lens_out, bounds_ref, zp, zq, length)
    if square:
        arrived(a_y + b_x + a_far + b_far)
        for p in range(gains_out.shape[0]):
            lanes = slice(p * shard, (p + 1) * shard)
            values = gains_out[p, :, :shard].astype(F32)
            gain_first[:, lanes] = values[0:1]
            second_ref[:, lanes] = values[3:4]
            half_pieces = gains_out.shape[0] // 2

            @pl.when(core == p // half_pieces)
            def _():
                at = (p % half_pieces) * shard
                gain_query[:, at : at + shard] = values[1:2]
                gain_key[:, at : at + shard] = values[2:3]
        weight = mix_out
    else:
        weight = mix_ref
        second_ref[...] = jnp.zeros_like(second_ref)
    writes = []

    def write(source, target, at):
        copy = pltpu.make_async_copy(source, target, write_sem.at[at])
        copy.start()
        writes.append(copy)

    query_out[0] = gain_query[...]
    query_out[1] = gain_first[:, : gain_query.shape[1]]
    key_out[0] = gain_key[...]
    key_out[1] = gain_first[:, gain_query.shape[1] :]
    write(weight, mix_hbm, 0)

    @pl.when(moves)
    def _():
        own_row.wait_recv()

    @pl.when(jnp.logical_not(moves))
    def _():
        stay_row.wait()

    first, second = 2 * core + zq, 2 * core + 1 - zq
    row_one = remote(quarter(row_ref, first), quarter(row_ref, first), sems, 3, partner)
    row_one.start()
    cross_row.wait_recv()
    row_two = remote(quarter(row_ref, second), quarter(row_ref, second), sems, 4, partner)
    row_two.start()

    def project(tokens, bufs):
        def one(i, _):
            rows = pl.ds(pl.multiple_of(i * BLOCK, BLOCK), BLOCK)
            project_kernel(
                tokens.at[rows], gain_first, weight, gain_query, gain_key, bufs["normed"].at[rows],
                bufs["q"].at[rows], bufs["k"].at[rows], bufs["v"].at[rows], bufs["raw"].at[rows],
            )
            return 0

        lax.fori_loop(0, length // BLOCK, one, 0)

    def attend(bufs, bounds):
        def one(p, _):
            lanes = pl.ds(pl.multiple_of(p * 128, 128), 128)
            attend_kernel(
                pics, bufs["q"].at[:, lanes], bufs["k"].at[:, lanes], bufs["v"].at[:, lanes], bounds,
                bufs["out"].at[:, lanes], bufs["aug"].at[pl.ds(2 * p, 2)], kaug, vaug, qaug.at[pl.ds(0, bufs["out"].shape[0])],
            )
            return 0

        lax.fori_loop(0, gain_query.shape[1] // 128, one, 0)

    row_one.wait_recv()
    row_two.wait_recv()
    project(row_ref, scratch[0])
    for i, name in enumerate(("normed", "k", "v", "raw")):
        write(scratch[0][name], outs[0][name], 1 + i)
    write(row_ref.at[rows_at(core * half, half)], x_out.at[pl.ds(0, half)], 5)

    @pl.when(moves)
    def _():
        own_shared.wait_recv()

    @pl.when(jnp.logical_not(moves))
    def _():
        stay_shared.wait()

    to_side = remote(quarter(shared_ref, first), quarter(shared_ref, first), sems, 5, side)
    to_side.start()
    shared_one = remote(quarter(shared_ref, first), quarter(shared_ref, first), sems, 6, partner)
    shared_one.start()
    cot_own = pl.ds(pl.multiple_of(zq * part, part), part)
    cot_shared = pl.ds(half, part)
    cot_moves = [
        remote(cot_ref.at[zq], cot_out.at[cot_own], sems, 46, keep),
        remote(cot_ref.at[2], cot_out.at[cot_shared], sems, 47, keep),
    ]
    cot_stays = [
        pltpu.make_async_copy(cot_ref.at[zq], cot_out.at[cot_own], local_sem.at[0]),
        pltpu.make_async_copy(cot_ref.at[2], cot_out.at[cot_shared], local_sem.at[1]),
    ]
    cot_cross = remote(cot_ref.at[1 - zq], cot_out.at[cot_own], sems, 48, cross)

    @pl.when(moves)
    def _():
        for copy in cot_moves:
            copy.start()

    @pl.when(jnp.logical_not(moves))
    def _():
        for copy in cot_stays:
            copy.start()

    cot_cross.start()
    attend(scratch[0], bounds_ref.at[0])
    write(scratch[0]["out"], outs[0]["out"], 6)
    write(scratch[0]["aug"], outs[0]["aug"], 7)
    to_side.wait_recv()
    shared_two = remote(quarter(shared_ref, second), quarter(shared_ref, second), sems, 7, partner)
    shared_two.start()
    if square:
        arrived(first_x + second_y)
        far_first = send_bundle(True, chip ^ 1, near_y)
        far_second = send_bundle(False, chip ^ 2, near_x)
    shared_one.wait_recv()
    shared_two.wait_recv()
    project(shared_ref, scratch[1])
    for i, name in enumerate(("normed", "k", "v", "raw")):
        write(scratch[1][name], outs[1][name], 8 + i)
    write(shared_ref.at[rows_at(first * part, part)], x_out.at[pl.ds(half, part)], 12)
    attend(scratch[1], bounds_ref.at[1])
    write(scratch[1]["out"], outs[1]["out"], 13)
    write(scratch[1]["aug"], outs[1]["aug"], 14)

    if square:
        arrived(first_y + second_x + far_first + far_second)
        sent_pieces = []
        for c in (chip ^ 1, chip ^ 2, chip ^ 3):
            target = block(outw_out, (2 * c + core) * shard, shard)
            sent_pieces.append(send(target, target, partner))
        write(up_out, up_hbm, 15)
        write(down_out, down_hbm, 16)
        arrived(sent_pieces + [out_core])
        write(outw_out, outw_hbm, 17)
        for copy in waits:
            copy.wait_send()
    cot_cross.wait()

    @pl.when(moves)
    def _():
        for copy in cot_moves:
            copy.wait()

    @pl.when(jnp.logical_not(moves))
    def _():
        for copy in cot_stays:
            copy.wait()

    write(cot_out, cot_hbm, 18)
    for copy in (row_one, row_two, shared_one, shared_two, to_side, cross_row):
        copy.wait_send()

    @pl.when(moves)
    def _():
        own_row.wait_send()
        own_shared.wait_send()

    for copy in writes:
        copy.wait()


def forward_pass(square, pics, tokens, cotangent, lens, mix, gains, *more):
    _, part, model = tokens.shape
    length, half, width = 4 * part, 2 * part, model // 2
    near = pl.BlockSpec(memory_space=pltpu.VMEM)
    anywhere = pl.BlockSpec(memory_space=pl.ANY)
    low = lambda *shape: (shape, BF16)
    wide = lambda *shape: (shape, F32)
    outs = [
        (low(3 * part, model), anywhere),
        (((2, 8, 128), jnp.int32), near),
        (low(model, 3 * width), anywhere),
        (wide(1, model), near),
        (wide(2, 1, width), near),
        (wide(2, 1, width), near),
        (low(3 * part, model), anywhere),
    ]
    bufs = []
    for queries in (length, half):
        shapes = [
            low(length, model), low(length, width), low(length, width), low(length, 2 * width),
            low(queries, width), low(2 * (width // 128), queries, 128),
        ]
        outs += [(shape, anywhere) for shape in shapes]
        bufs += shapes + [low(length, width)]
    scratch = [low(length, model), low(length, model), low(3 * part, model), ((2,) + lens.shape, jnp.int32)] + bufs
    scratch += [low(2, length, 128), low(2, length, 128), low(length, 128)]
    if square:
        up, down, outw = more
        landed = [low(model, up.shape[2]), low(4 * down.shape[0], model), low(model, model)]
        outs += [(shape, anywhere) for shape in landed]
        scratch += [low(model, 3 * width), low(8, *gains.shape), wide(1, model), wide(1, width), wide(1, width)]
        scratch += landed
    return pl.pallas_call(
        functools.partial(forward_kernel, square, pics),
        in_specs=[near] * (5 + len(more)),
        out_specs=[spec for _, spec in outs],
        out_shape=[jax.ShapeDtypeStruct(*shape) for shape, _ in outs],
        scratch_shapes=[pltpu.VMEM(*shape) for shape in scratch]
        + [
            pltpu.SemaphoreType.DMA((49,)),
            pltpu.SemaphoreType.DMA((49,)),
            pltpu.SemaphoreType.DMA((8,)),
            pltpu.SemaphoreType.DMA((19,)),
        ],
        compiler_params=pltpu.CompilerParams(
            collective_id=0, has_side_effects=True, vmem_limit_bytes=60 * 1024 * 1024
        ),
        name="forward_pass",
    )(tokens, cotangent, lens, mix, gains, *more)


def dense_kernel(
    out_ref, shared_ref, x, grad_ref, outw_ref, gain_ref,
    bounds_ref, up_ref, down_ref,
    out_keep, out_cross, out_third, midg_ref, row_grad, shared_grad, packed, gaing_ref,
    att_other, second, grad, hidden_all, pre_all, forward, backward, middle, ups, downs,
    parts_out, parts_in, heads_out, cols_out, cols_in, sent, got, tile_sem,
):
    chip, core, zp, zq = here()
    sems = (sent, got)
    partner = (chip, 1 - core, zp, zq)
    tokens, model = midg_ref.shape
    part = tokens // 3
    half = 2 * part
    width = out_ref.shape[1]
    tile = ups.shape[2]
    other = 1 - core
    mine, theirs = pl.ds(0, tokens), pl.ds(tokens, tokens)

    for i in range(4):
        pltpu.make_async_copy(up_ref.at[:, pl.ds(i * tile, tile)], ups.at[i], tile_sem.at[0, i]).start()
        pltpu.make_async_copy(down_ref.at[pl.ds(i * tile, tile)], downs.at[i], tile_sem.at[1, i]).start()
    greet([partner])
    att_sends = [
        remote(out_ref.at[rows_at(other * half, half)], att_other.at[pl.ds(0, half)], sems, 0, partner),
        remote(shared_ref.at[rows_at(other * part, part)], att_other.at[pl.ds(half, part)], sems, 1, partner),
    ]
    for copy in att_sends:
        copy.start()

    slot = lax.broadcasted_iota(jnp.int32, (part, 1), 0)
    filled, shared_filled = bounds_ref[0, 3:4, 0:1], bounds_ref[1, 3:4, 0:1]
    none = jnp.zeros((), BF16)
    for b, start, limit in (
        (0, 2 * core * part, filled),
        (1, (2 * core + 1) * part, filled),
        (2, (2 * core + zq) * part, shared_filled),
    ):
        rows = pl.ds(b * part, part)
        grad[rows, :] = jnp.where(slot + start < limit, grad_ref[rows, :], none)
    grad_send = remote(grad.at[mine], grad.at[theirs], sems, 2, partner)
    grad_send.start()

    own_rows_of = lambda b: (
        out_ref[rows_at(core * half + b * part, part), :] if b < 2 else shared_ref[rows_at(core * part, part), :]
    )
    own_weight = outw_ref[rows_at(core * width, width), :]
    other_weight = outw_ref[rows_at(other * width, width), :]
    blocks = [pl.ds(b * part, part) for b in range(3)]
    for b in range(3):
        middle[blocks[b], :] = x[blocks[b], :].astype(F32) + jnp.dot(
            own_rows_of(b), own_weight, preferred_element_type=F32
        )
    for copy in att_sends:
        copy.wait_recv()
    for rows in blocks:
        value = middle[rows, :] + jnp.dot(att_other[rows, :], other_weight, preferred_element_type=F32)
        middle[rows, :] = value
        second[rows, :] = (norm_parts(value)[0] * gain_ref[...]).astype(BF16)
    second_send = remote(second.at[mine], second.at[theirs], sems, 3, partner)
    second_send.start()
    forward[...] = jnp.zeros_like(forward)
    backward[...] = jnp.zeros_like(backward)
    second_send.wait_recv()
    grad_send.wait_recv()

    def one_tile(i, _):
        pltpu.make_async_copy(up_ref.at[:, pl.ds(0, tile)], ups.at[i], tile_sem.at[0, i]).wait()
        pltpu.make_async_copy(down_ref.at[pl.ds(0, tile)], downs.at[i], tile_sem.at[1, i]).wait()
        up, down = ups[i], downs[i]
        for rows in (mine, theirs):
            pre = jnp.dot(second[rows, :], up, preferred_element_type=F32)
            hidden, slope = gelu_pair(pre)
            hidden = hidden.astype(BF16)
            hidden_all[rows, :] = hidden
            forward[rows, :] += jnp.dot(hidden, down, preferred_element_type=F32)
            pre_grad = (nt(grad[rows, :], down) * slope).astype(BF16)
            pre_all[rows, :] = pre_grad
            backward[rows, :] += nt(pre_grad, up)
        packed[i, pl.ds(0, tile), :] = tn(hidden_all[...], grad[...]).astype(BF16)
        up_grad = tn(second[...], pre_all[...]).astype(BF16)
        quarter = model // 4
        for c in range(4):
            place = (rows_at(tile + (i // 2) * quarter, quarter), pl.ds(pl.multiple_of((i % 2) * tile, 128), tile))
            packed[c, place[0], place[1]] = up_grad[c * quarter : (c + 1) * quarter, :]
        return 0

    lax.fori_loop(0, 4, one_tile, 0)

    parts_out[0] = forward[theirs, :].astype(BF16)
    first_part = remote(parts_out.at[0], parts_in.at[0], sems, 4, partner)
    first_part.start()
    parts_out[1] = backward[theirs, :].astype(BF16)
    second_part = remote(parts_out.at[1], parts_in.at[1], sems, 5, partner)
    second_part.start()
    second_send.wait_send()
    first_part.wait_recv()
    for rows in blocks:
        value = middle[rows, :] + forward[rows, :] + parts_in[0, rows, :].astype(F32)
        forward[rows, :] = value
    out_keep[...] = forward[rows_at(zq * part, part), :].astype(BF16)
    out_cross[...] = forward[rows_at((1 - zq) * part, part), :].astype(BF16)
    out_third[...] = forward[pl.ds(half, part), :].astype(BF16)
    second_part.wait_recv()
    gain_sum = jnp.zeros(gaing_ref.shape, F32)
    for b in range(3):
        rows = blocks[b]
        n, r = norm_parts(middle[rows, :])
        upstream = backward[rows, :] + parts_in[1, rows, :].astype(F32)
        more, gain_more = norm_back(upstream, n, r, gain_ref[...])
        gain_sum = gain_sum + gain_more
        value = grad[rows, :].astype(F32) + more
        midg_ref[rows, :] = value
        branch = value.astype(BF16)
        second[rows, :] = branch
        heads_out[rows, :] = nt(branch, other_weight).astype(BF16)
    gaing_ref[...] = gain_sum
    head_sends = [
        remote(heads_out.at[pl.ds(0, half)], row_grad.at[rows_at(core * half, half)], sems, 6, partner),
        remote(heads_out.at[pl.ds(half, part)], shared_grad.at[rows_at(core * part, part)], sems, 7, partner),
    ]
    for copy in head_sends:
        copy.start()
    branch = second[mine, :]
    out_grads = [
        tn(out_ref[rows_at(core * half, half), :], second[pl.ds(0, half), :])
        + tn(shared_ref[rows_at(core * part, part), :], second[pl.ds(half, part), :]),
        tn(att_other[...], branch),
    ]
    for turn, heads in ((0, core), (1, other)):
        rows = rows_at(heads * width, width)
        forward[rows, :] = out_grads[turn]
    lanes = lambda side: pl.ds(pl.multiple_of(side * width, 128), width)
    cols_out[...] = forward[pl.ds(0, model), lanes(other)].astype(BF16)
    cols_send = remote(cols_out, cols_in, sems, 8, partner)
    cols_send.start()
    for b in range(3):
        value = nt(second[blocks[b], :], own_weight).astype(BF16)
        if b < 2:
            row_grad[rows_at(core * half + b * part, part), :] = value
        else:
            shared_grad[rows_at(core * part, part), :] = value
    cols_send.wait_recv()
    total = (forward[pl.ds(0, model), lanes(core)] + cols_in[...].astype(F32)).astype(BF16)
    eighth = model // 8
    for c in range(4):
        for h in range(2):
            at = (2 * c + h) * eighth
            packed[c, pl.ds(2 * tile, eighth), h * width : (h + 1) * width] = total[at : at + eighth, :]
    for copy in head_sends:
        copy.wait_recv()
    for copy in att_sends + head_sends + [grad_send, first_part, second_part, cols_send]:
        copy.wait_send()


def dense(out, shared_out, x, grad, out_matrix, gain, bounds, up, down):
    model = x.shape[1]
    tokens = x.shape[0]
    part = tokens // 3
    length, width = out.shape
    hidden = down.shape[0]
    tile = hidden // 4
    anywhere = pl.BlockSpec(memory_space=pl.ANY)
    near = pl.BlockSpec(memory_space=pltpu.VMEM)
    both = 2 * tokens
    return pl.pallas_call(
        dense_kernel,
        in_specs=[near] * 7 + [anywhere, anywhere],
        out_specs=[near] * 8,
        out_shape=[
            jax.ShapeDtypeStruct((part, model), BF16),
            jax.ShapeDtypeStruct((part, model), BF16),
            jax.ShapeDtypeStruct((part, model), BF16),
            jax.ShapeDtypeStruct((tokens, model), F32),
            jax.ShapeDtypeStruct((length, width), BF16),
            jax.ShapeDtypeStruct((length // 2, width), BF16),
            jax.ShapeDtypeStruct((4, 2 * tile + model // 8, model), BF16),
            jax.ShapeDtypeStruct((1, model), F32),
        ],
        scratch_shapes=[
            pltpu.VMEM((tokens, width), BF16),
            pltpu.VMEM((both, model), BF16),
            pltpu.VMEM((both, model), BF16),
            pltpu.VMEM((both, tile), BF16),
            pltpu.VMEM((both, tile), BF16),
            pltpu.VMEM((both, model), F32),
            pltpu.VMEM((both, model), F32),
            pltpu.VMEM((tokens, model), F32),
            pltpu.VMEM((4, model, tile), BF16),
            pltpu.VMEM((4, tile, model), BF16),
            pltpu.VMEM((2, tokens, model), BF16),
            pltpu.VMEM((2, tokens, model), BF16),
            pltpu.VMEM((tokens, width), BF16),
            pltpu.VMEM((model, width), BF16),
            pltpu.VMEM((model, width), BF16),
            pltpu.SemaphoreType.DMA((9,)),
            pltpu.SemaphoreType.DMA((9,)),
            pltpu.SemaphoreType.DMA((2, 4)),
        ],
        compiler_params=pltpu.CompilerParams(
            collective_id=1, has_side_effects=True, vmem_limit_bytes=60 * 1024 * 1024
        ),
        cost_estimate=pl.CostEstimate(
            flops=32 * tokens * model * hidden, bytes_accessed=16 * model * hidden, transcendentals=0
        ),
        name="dense",
    )(out, shared_out, x, grad, out_matrix, gain, bounds, up, down)


def finish_kernel(
    grad_ref, mix_ref, out_ref, total_ref, gains_ref,
    relay, final, core_got, chunks, gain_parts, chunk_got, gain_got, sent, got, local_sem,
):
    chip, core, zp, zq = here()
    z = 2 * zp + zq
    sems = (sent, got)
    part = out_ref.shape[1]
    shard = mix_ref.shape[1] - 16
    quarter = shard // 2
    columns = mix_ref.shape[2]
    partner = (chip, 1 - core, zp, zq)
    keep = (chip, zp, core, zq)
    cross = (chip, zp, core, 1 - zq)
    moves = core != zp
    near_x = (chip ^ 1, core, zp, zq)
    near_y = (chip ^ 2, core, zp, zq)
    along = [(chip, core, zp, 1 - zq), (chip, core, 1 - zp, zq), (chip, core, 1 - zp, 1 - zq)]
    greet([partner, cross, near_x, near_y] + along, keep, moves)

    mine, theirs = 2 * chip + core, 2 * chip + 1 - core
    x_mine, x_other = 2 * (chip ^ 1) + core, 2 * (chip ^ 1) + 1 - core
    y_mine, y_other = 2 * (chip ^ 2) + core, 2 * (chip ^ 2) + 1 - core
    far_mine, far_other = 2 * (chip ^ 3) + core, 2 * (chip ^ 3) + 1 - core
    first = remote(mix_ref.at[far_mine], relay.at[0], sems, 0, near_y)
    second = remote(mix_ref.at[far_other], relay.at[1], sems, 1, near_x)
    first.start()
    second.start()
    direct_x = remote(mix_ref.at[x_other], final.at[0], sems, 2, near_x)
    direct_y = remote(mix_ref.at[y_mine], final.at[1], sems, 3, near_y)
    direct_x.start()
    direct_y.start()

    own = pl.ds(pl.multiple_of(zq * part, 16), part)
    own_row = remote(grad_ref.at[own], out_ref.at[zq], sems, 4, keep)
    own_shared = remote(grad_ref.at[pl.ds(2 * part, part)], out_ref.at[2], sems, 5, keep)
    stay_row = pltpu.make_async_copy(grad_ref.at[own], out_ref.at[zq], local_sem.at[0])
    stay_shared = pltpu.make_async_copy(grad_ref.at[pl.ds(2 * part, part)], out_ref.at[2], local_sem.at[1])

    @pl.when(moves)
    def _():
        own_row.start()
        own_shared.start()

    @pl.when(jnp.logical_not(moves))
    def _():
        stay_row.start()
        stay_shared.start()

    cross_row = remote(grad_ref.at[rows_at((1 - zq) * part, part)], out_ref.at[zq], sems, 6, cross)
    cross_row.start()

    def add(*terms):
        total = terms[0].astype(F32)
        for term in terms[1:]:
            total = total + term.astype(F32)
        return total

    first.wait_recv()
    relay[2] = add(relay[0], mix_ref[x_mine]).astype(BF16)
    onward_x = remote(relay.at[2], final.at[2], sems, 7, near_x)
    onward_x.start()
    second.wait_recv()
    relay[3] = add(relay[1], mix_ref[y_other]).astype(BF16)
    onward_y = remote(relay.at[3], final.at[3], sems, 8, near_y)
    onward_y.start()
    direct_x.wait_recv()
    onward_y.wait_recv()
    relay[4] = add(mix_ref[theirs], final[0], final[3]).astype(BF16)
    to_core = remote(relay.at[4], core_got, sems, 9, partner)
    to_core.start()
    direct_y.wait_recv()
    onward_x.wait_recv()
    kept = add(mix_ref[mine], final[1], final[2])
    for i in range(2):
        chunks[2 * core + i] = kept[i * quarter : (i + 1) * quarter].astype(BF16)
    to_core.wait_recv()
    for i in range(2):
        chunks[2 * (1 - core) + i] = core_got[i * quarter : (i + 1) * quarter]
    gain_parts[0] = (kept[shard:] + core_got[shard:].astype(F32)).astype(BF16)
    hops = [z ^ 1, z ^ 2, z ^ 3]
    copies = []
    for i in range(3):
        copies.append(remote(chunks.at[hops[i]], chunk_got.at[i], sems, 10 + i, along[i]))
        copies.append(remote(gain_parts.at[0], gain_got.at[i], sems, 13 + i, along[i]))
    for copy in copies:
        copy.start()
    for copy in copies:
        copy.wait_recv()
    gains_ref[...] = add(gain_parts[0], gain_got[0], gain_got[1], gain_got[2])
    chunk_got[3] = add(chunks[z], chunk_got[0], chunk_got[1], chunk_got[2]).astype(BF16)
    spread = [remote(chunk_got.at[3], chunk_got.at[4 + i], sems, 16 + i, along[i]) for i in range(3)]
    for copy in spread:
        copy.start()

    def place(index, values):
        half, up = index // 2, index % 2
        third = columns // 3
        values = values.astype(F32)
        for h in range(2):
            for u in range(2):

                @pl.when((half == h) & (up == u))
                def _():
                    for p in range(3):
                        total_ref[u * quarter : (u + 1) * quarter, (2 * p + h) * third : (2 * p + h + 1) * third] = (
                            values[:, p * third : (p + 1) * third]
                        )

    place(z, chunk_got[3])
    for i in range(3):
        spread[i].wait_recv()
        place(hops[i], chunk_got[4 + i])
    for copy in copies + spread + [first, second, direct_x, direct_y, onward_x, onward_y, to_core]:
        copy.wait_send()
    cross_row.wait()

    @pl.when(moves)
    def _():
        own_row.wait()
        own_shared.wait()

    @pl.when(jnp.logical_not(moves))
    def _():
        stay_row.wait()
        stay_shared.wait()


def finish(grad, mix):
    tokens, model = grad.shape
    _, rows, columns = mix.shape
    shard = rows - 16
    local_space = pl.BlockSpec(memory_space=pltpu.VMEM)
    buffers = lambda count, size: pltpu.VMEM((count, size, columns), BF16)
    return pl.pallas_call(
        finish_kernel,
        in_specs=[local_space, local_space],
        out_specs=[local_space, local_space, local_space],
        out_shape=[
            jax.ShapeDtypeStruct((3, tokens // 3, model), BF16),
            jax.ShapeDtypeStruct((shard, 2 * columns), F32),
            jax.ShapeDtypeStruct((16, columns), F32),
        ],
        scratch_shapes=[
            buffers(5, rows),
            buffers(4, rows),
            pltpu.VMEM((rows, columns), BF16),
            buffers(4, shard // 2),
            buffers(1, 16),
            buffers(7, shard // 2),
            buffers(3, 16),
            pltpu.SemaphoreType.DMA((19,)),
            pltpu.SemaphoreType.DMA((19,)),
            pltpu.SemaphoreType.DMA((2,)),
        ],
        compiler_params=pltpu.CompilerParams(
            collective_id=3, has_side_effects=True, vmem_limit_bytes=VMEM_LIMIT
        ),
        name="finish",
    )(grad, mix)


def local(
    tokens, lengths, pictures, first_gain, mix_weight, query_gain, key_gain, out_weight,
    second_gain, up_weight, down_weight, cotangent,
):
    chip, core, zp, zq = here()
    chips = lax.axis_size("chip")
    square = chips == 4
    rows = ("chip", "core")
    _, part, model = tokens.shape
    length = 4 * part
    half = 2 * part
    width = HEADS // 2 * HEAD
    pics = lengths.shape[1]
    shard = mix_weight.shape[0]

    gains = jnp.stack([first_gain, query_gain, key_gain, second_gain])
    gains = jnp.pad(gains, ((0, 12), (0, 128 - shard)))
    mix_split = mix_weight.reshape(shard, 3, 2, width).transpose(2, 0, 1, 3).reshape(2, shard, 3 * width)
    lens = jnp.pad(lengths, ((0, 5), (0, 128 - pics)))
    hidden = up_weight.shape[1]
    tile = hidden // 8
    if square:
        up_split = up_weight.reshape(shard, 4, 2, tile).transpose(2, 0, 1, 3).reshape(2, shard, 4 * tile)
        forward = forward_pass(
            True, pics, tokens, cotangent, lens, mix_split, gains, up_split, down_weight, out_weight
        )
        up_half, down_half, out_matrix = forward[19:]
        gain_second = forward[3]
    else:
        gather = lambda weight: lax.all_gather(weight, rows, axis=0, tiled=True)
        half_of = lambda weight, axis: pick(weight, core, axis)
        mix_half = half_of(gather(mix_weight).reshape(model, 3, 2, width), 2).reshape(model, 3 * width)
        up_half = half_of(gather(up_weight).reshape(model, 4, 2, tile), 2).reshape(model, 4 * tile)
        down_half = half_of(gather(down_weight).reshape(4, 2, tile, model), 1).reshape(4 * tile, model)
        out_matrix = gather(out_weight)
        spread_gains = lax.all_gather(gains, rows, axis=0, tiled=False)
        spread_gains = spread_gains[:, :4, :shard].transpose(1, 0, 2).reshape(4, 1, model).astype(F32)
        gain_second = spread_gains[3]
        forward = forward_pass(
            False, pics, tokens, cotangent, lens, mix_half, gains, spread_gains[0],
            half_of(spread_gains[1].reshape(2, 1, width), 0), half_of(spread_gains[2].reshape(2, 1, width), 0),
        )
    own_tokens, bounds, mix_half, _, query_first, key_first, grad_tokens = forward[:7]
    gain_query, gain_key = query_first[0], key_first[0]
    gain_first = jnp.concatenate([query_first[1], key_first[1]], axis=1)
    normed, k, v, raw, out, aug = forward[7:13]
    shared_normed, shared_k, shared_v, shared_raw, shared_out, shared_aug = forward[13:19]

    def collect(mine, cross, third):
        mine = lax.ppermute(mine, COLUMN, KEEP)
        cross = lax.ppermute(cross, COLUMN, CROSS)
        third = lax.ppermute(third, COLUMN, KEEP)
        return jnp.stack([jnp.where(zq == 0, mine, cross), jnp.where(zq == 0, cross, mine), third])

    out_keep, out_cross, out_third, middle_grad, grad, shared_grad, packed, second_gain_grad = dense(
        out, shared_out, own_tokens, grad_tokens, out_matrix, gain_second, bounds, up_half, down_half
    )
    output = collect(out_keep, out_cross, out_third)

    def reduce(grad):
        return lax.psum(lax.psum_scatter(grad, rows, scatter_dimension=0, tiled=True), SEQ).astype(F32)

    eighth = model // 8
    if square:
        size = packed.shape[1]
        mine = lax.psum_scatter(packed.reshape(4 * size, model), "chip", scatter_dimension=0, tiled=True)
        mine = lax.psum(mine, SEQ)
        down_out = mine[:tile].astype(F32)
        up_mine = mine[tile : 2 * tile].reshape(2, 2, shard, 2, tile).transpose(1, 2, 0, 3, 4)
        up_mine = up_mine.reshape(2, shard, 4, tile)
        outw_mine = mine[2 * tile :].reshape(shard, 2, width).transpose(1, 0, 2)
        up_other = swap(pick(up_mine, 1 - core).reshape(shard, 4 * tile), "core").reshape(shard, 4, tile)
        outw_other = swap(pick(outw_mine, 1 - core), "core")
        up_mine, outw_mine = pick(up_mine, core), pick(outw_mine, core)
        low = jnp.where(core == 0, up_mine, up_other)
        high = jnp.where(core == 0, up_other, up_mine)
        up_out = jnp.stack([low, high], axis=2).reshape(shard, hidden).astype(F32)
        low = jnp.where(core == 0, outw_mine, outw_other)
        high = jnp.where(core == 0, outw_other, outw_mine)
        outw_out = jnp.concatenate([low, high], axis=1).astype(F32)
    else:
        own_core = jnp.arange(2) == core
        down_grad = packed[:, None, :tile]
        down_out = reduce(jnp.where(own_core[None, :, None, None], down_grad, 0).reshape(hidden, model))
        up_grad = packed[:, tile : 2 * tile].reshape(4, 2, 2 * eighth, 2, tile).transpose(0, 2, 1, 3, 4)
        up_grad = up_grad.reshape(model, 4, 1, tile)
        up_out = reduce(jnp.where(own_core[None, None, :, None], up_grad, 0).reshape(model, hidden))
        out_grad = packed[:, 2 * tile :].reshape(4, eighth, 2, width).transpose(0, 2, 1, 3)
        out_grad = out_grad.reshape(model, 1, width)
        outw_out = reduce(jnp.where(own_core[None, :, None], out_grad, 0).reshape(model, model))

    shared_dq, part_k, part_v, shared_qgg, _ = attend_back(
        shared_aug, shared_k, shared_v, shared_out, shared_grad, shared_raw, gain_query, gain_key,
        bounds[1], pics,
    )

    def to_side(array):
        return swap(pick(array.reshape(2, 2, part, width), 1 - zq, 1), "zq").reshape(half, width)

    got_k, got_v = to_side(part_k), to_side(part_v)
    dq, dk, dv, qgg, kgg = attend_back(
        aug, k, v, out, grad, raw, gain_query, gain_key, bounds[0], pics
    )
    shared_dk, shared_dv, shared_kgg = shared_keys(part_k, part_v, got_k, got_v, shared_raw, gain_key)
    mixed = jnp.concatenate(
        [jnp.concatenate([dq, shared_dq]), jnp.concatenate([dk, shared_dk]), jnp.concatenate([dv, shared_dv])],
        axis=1,
    )
    own_shared = pick(shared_normed.reshape(2, 2, part, model), zq, 1).reshape(half, model)
    mix_grad = tn(jnp.concatenate([normed, own_shared]), mixed).astype(BF16)
    partial = nt(mixed, mix_half)
    row_partial = partial[:length].reshape(2, half, model)
    shared_partial = partial[length:].reshape(2, part, model)
    mine = jnp.concatenate([pick(row_partial, core), pick(shared_partial, core)])
    sent = jnp.concatenate([pick(row_partial, 1 - core), pick(shared_partial, 1 - core)])
    normed_grad = mine + swap(sent.astype(BF16), "core").astype(F32)
    n_first, r_first = norm_parts(own_tokens.astype(F32))
    input_part, first_gain_grad = norm_back(normed_grad, n_first, r_first, gain_first)
    input_grad = (middle_grad + input_part).astype(BF16)

    def place_heads(values):
        return jnp.where(jnp.arange(2)[:, None] == core, values, 0.0).reshape(1, model)

    gain_grads = jnp.concatenate(
        [first_gain_grad, place_heads(qgg + shared_qgg), place_heads(kgg + shared_kgg), second_gain_grad]
    )
    gain_grads = gain_grads.reshape(4, 2 * chips, shard).transpose(1, 0, 2).astype(BF16)
    if square:
        gain_rows = jnp.pad(gain_grads, ((0, 0), (0, 12), (0, 3 * width - shard)))
        payload = jnp.concatenate([mix_grad.reshape(2 * chips, shard, 3 * width), gain_rows], axis=1)
        input_out, mix_out, gains_out = finish(input_grad, payload)
        gains_out = gains_out[:4, :shard]
    else:
        first, second = input_grad[:part], input_grad[part:half]
        input_out = collect(
            jnp.where(zq == 0, first, second), jnp.where(zq == 0, second, first), input_grad[half:]
        )
        spread_mix = jnp.where(
            jnp.arange(2)[None, None, :, None] == core, mix_grad.reshape(model, 3, 1, width), 0
        ).reshape(model, 6 * width)
        mix_out = reduce(spread_mix)
        gains_out = reduce(gain_grads).reshape(4, shard)
    return (
        output, input_out, gains_out[0], mix_out, gains_out[1], gains_out[2], outw_out, gains_out[3],
        up_out, down_out,
    )


def solution(mesh):
    fsdp = mesh.shape["fsdp"]
    split = Mesh(mesh.devices.reshape(fsdp // 2, 2, 2, 2), ("chip", "core", "zp", "zq"))
    rows = ("chip", "core")
    return jax.shard_map(
        local,
        mesh=split,
        in_specs=(
            P(rows, SEQ, None),
            P(rows, None),
            P(rows, SEQ),
            P(rows),
            P(rows, None),
            P(rows),
            P(rows),
            P(rows, None),
            P(rows),
            P(rows, None),
            P(rows, None),
            P(rows, SEQ, None),
        ),
        out_specs=(
            P(rows, SEQ, None),
            P(rows, SEQ, None),
            P(rows),
            P(rows, None),
            P(rows),
            P(rows),
            P(rows, None),
            P(rows),
            P(rows, None),
            P(rows, None),
        ),
        check_vma=False,
    )
```

profile of v0, /device:TPU:0, one launch (start us, length us, event | category | flops | bytes accessed | tf_op | source)
XLA Modules:
  0.0 358.6 jit_solution(15797832282366106816)
XLA Ops:
  7.2 1.2 reshape.236
  12.8 76.6 %forward_pass.1 = (bf16[768,768]{1,0:T(8,128)(2,1)}, s32[2,8,128]{2,1,0:T(8,128)}, bf16[768,1152]{1,0:T(8,128)(2,1)}, f32[1,768]{1,0:T(1,128)}, f32[2,1,384]{2,1...) custom-call(bf16[3,256,768]{2,1,0:T(8,128)(2,1)} %refs_0_.1, ...), custom_call_target="tpu_custom_call" | custom-call | tf_op jit(solution)/shard_map/forward_pass/pallas_call | solution.py:734
  89.4 56.3 %dense.1 = (bf16[256,768]{1,0:T(8,128)(2,1)}, bf16[256,768]{1,0:T(8,128)(2,1)}, bf16[256,768]{1,0:T(8,128)(2,1)}, f32[768,768]{1,0:T(8,128)}, bf16[1024,384]{1,0...) custom-call(bf16[1024,384]{1,0:T(8,128)(2,1)} %get-tuple-element.55.out_ref, ...), custom_call_target="tpu_custom_call" | custom-call | flops 28991029248 | bytes 18874368 | tf_op jit(solution)/shard_map/dense/pallas_call | solution.py:917
  147.7 12.7 %attend_back.3 = (bf16[512,384]{1,0:T(8,128)(2,1)}, bf16[1024,384]{1,0:T(8,128)(2,1)}, bf16[1024,384]{1,0:T(8,128)(2,1)}, f32[1,384]{1,0:T(1,128)}, f32[1,384]{1,0:T(1,128)}) custom-call(bf16[6,512,128]{2,1,0:T(8,128)(2,1)} %get-tuple-element.76.aug_ref, bf16[1024,384]{1,0:T(8,128)(2,1)} %get-tuple-element.77.k_ref, ...), custom_call_target="tpu_custom_call" | custom-call | flops 8053063680 | bytes 7864320 | tf_op jit(solution)/shard_map/attend_back/pallas_call | solution.py:241
  162.5 2.1 collective-permute-start.4
  164.6 1.6 collective-permute-start
  166.3 1.7 collective-permute-start.2
  168.6 24.9 %attend_back.2 = (bf16[1024,384]{1,0:T(8,128)(2,1)}, bf16[1024,384]{1,0:T(8,128)(2,1)}, bf16[1024,384]{1,0:T(8,128)(2,1)}, f32[1,384]{1,0:T(1,128)}, f32[1,384]{1,0:T(1,128)}) custom-call(bf16[6,1024,128]{2,1,0:T(8,128)(2,1)} %get-tuple-element.68.aug_ref, bf16[1024,384]{1,0:T(8,128)(2,1)} %get-tuple-element.69.k_ref, ...), custom_call_target="tpu_custom_call" | custom-call | flops 16106127360 | bytes 7864320 | tf_op jit(solution)/shard_map/attend_back/pallas_call | solution.py:241
  195.8 2.1 constant_dynamic-slice_fusion.3
  199.6 4.5 %shared_keys.1 = (bf16[512,384]{1,0:T(8,128)(2,1)}, bf16[512,384]{1,0:T(8,128)(2,1)}, f32[1,384]{1,0:T(1,128)}) custom-call(bf16[1024,384]{1,0:T(8,128)(2,1)} %get-tuple-element.83.dk_ref, bf16[1024,384]{1,0:T(8,128)(2,1)} %get-tuple-element.84.dv_ref, bf16[512,384]{1,0:T(8,128)(2,1)} %bitcast.92, bf16[512,384]{1,0:T(8,128)(2,1)} %bitcast.93, ...), custom_call_target="tpu_custom_call" | custom-call | tf_op jit(solution)/shard_map/shared_keys/pallas_call | solution.py:300
  204.2 13.6 %fusion.34 = f32[1536,768]{1,0:T(8,128)S(1)} fusion(bf16[768,1152]{1,0:T(8,128)(2,1)S(1)} %copy-done.27, bf16[512,384]{1,0:T(8,128)(2,1)} %get-tuple-element.87, bf16[1024,384]{1,0:T(8,128)(2,1)S(1)} %copy-done.35, bf16[512,384]{1,0:T(8,128)(2,1)} %get-tuple-element.85, bf16[1024,384]{1,0:T(8,128)(2,1)S(1)} %copy-done.33, ...), kind=kOutput, calls=%fused_computation.89 | convolution fusion | flops 2739142656 | bytes 10027008 | tf_op jit(solution)/shard_map/dot_general | solution.py:75
  217.9 2.1 slice.65
  220.6 1.3 broadcast_in_dim.55
  222.0 1.5 fusion.17
  223.6 5.9 %collective-permute-start.5 = (bf16[768,768]{1,0:T(8,128)(2,1)S(1)}, bf16[768,768]{1,0:T(8,128)(2,1)S(1)}, u32[]{:S(2)}, u32[]{:S(2)}) collective-permute-start(bf16[768,768]{1,0:T(8,128)(2,1)S(1)} %pad_maximum_fusion.1), channel_id=1, source_target_pairs={{0,4},{4,0},{1,5},{5,1},{2,6},{6,2},{3,7},{7,3},{8,12},{12,8},{9,1... | collective-permute-start | bytes 3538952 | tf_op jit(solution)/shard_map/ppermute | solution.py:33
  233.8 4.6 %convolution_convert_fusion = bf16[768,1152]{1,0:T(8,128)(2,1)} fusion(bf16[512,768]{1,0:T(8,128)(2,1)S(1)} %bitcast.90, bf16[1024,768]{1,0:T(8,128)(2,1)S(1)} %copy-done.28, bf16[512,384]{1,0:T(8,128)(2,1)S(1)} %copy-done.30, bf16[1024,384]{1,0:T(8,128)(2,1)S(1)} %copy-done.36, bf16[512,384]{1,0:T(8,128)(2,1)S(1)} %copy-done.29, ...), kind=kOutput, calls=%fused_computation.3 | convolution fusion | flops 2744745984 | bytes 7667712 | tf_op jit(solution)/shard_map/dot_general | solution.py:79
  239.5 1.8 fusion.11
  242.0 1.4 concatenate.53
  245.3 3.0 fusion.16.mix_ref
  248.3 2.2 fusion.10.grad_ref
  250.5 88.3 %finish.1 = (bf16[3,256,768]{2,1,0:T(8,128)(2,1)}, f32[96,2304]{1,0:T(8,128)}, f32[16,1152]{1,0:T(8,128)}) custom-call(bf16[768,768]{1,0:T(8,128)(2,1)} %fusion.10.grad_ref, bf16[8,112,1152]{2,1,0:T(8,128)(2,1)} %fusion.16.mix_ref), custom_call_target="tpu_custom_call" | custom-call | tf_op jit(solution)/shard_map/finish/pallas_call | solution.py:1095
  338.8 1.4 slice_bitcast_fusion.6
  341.5 2.4 slice_convert_fusion
  347.4 2.0 reshape.255
  (150 shorter events, 28.4 us)
Async XLA Ops:
  7.2 234.1 %reduce-scatter.2.cloned.1.call-start = ((), (), s32[]{:S(2)}) async-start(), calls=%async_computation.1 | async-start | bytes 6635520 | tf_op jit(solution)/shard_map/reduce_scatter | solution.py:1188
  145.8 194.3 %all-reduce.5.cloned.1.call-start = ((), (), s32[]{:S(2)}) async-start(), calls=%async_computation.2 | async-start | bytes 2654208 | tf_op jit(solution)/shard_map/psum | solution.py:1189
  161.4 37.3 %collective-permute-start.3 = (bf16[2,256,384]{2,1,0:T(8,128)(2,1)S(1)}, bf16[2,256,384]{2,1,0:T(8,128)(2,1)S(1)}, u32[]{:S(2)}, u32[]{:S(2)}) collective-permute-start(bf16[2,256,384]{2,1,0:T(8,128)(2,1)S(1)} %dynamic-slice_bitcast_fusion.3), channel_id=1, source_target_pairs={{0,1},{1,0},{2,3},{3,2},{4,5},{5,4},{6,7},{7,6},{8,9},{9,8},{10,11... | collective-permute-start | bytes 1179656 | tf_op jit(solution)/shard_map/ppermute | solution.py:33
  162.5 36.2 %collective-permute-start.4 = (bf16[2,256,384]{2,1,0:T(8,128)(2,1)S(1)}, bf16[2,256,384]{2,1,0:T(8,128)(2,1)S(1)}, u32[]{:S(2)}, u32[]{:S(2)}) collective-permute-start(bf16[2,256,384]{2,1,0:T(8,128)(2,1)S(1)} %dynamic-slice_bitcast_fusion.2), channel_id=1, source_target_pairs={{0,1},{1,0},{2,3},{3,2},{4,5},{5,4},{6,7},{7,6},{8,9},{9,8},{10,11... | collective-permute-start | bytes 1179656 | tf_op jit(solution)/shard_map/ppermute | solution.py:33
  164.6 64.9 %collective-permute-start = (bf16[256,768]{1,0:T(8,128)(2,1)}, bf16[256,768]{1,0:T(8,128)(2,1)S(1)}, u32[]{:S(2)}, u32[]{:S(2)}) collective-permute-start(bf16[256,768]{1,0:T(8,128)(2,1)} %get-tuple-element.64), channel_id=1, source_target_pairs={{0,0},{1,1},{2,4},{3,5},{4,2},{5,3},{6,6},{7,7},{8,8},{9,9},{10,12... | collective-permute-start | bytes 1179656 | tf_op jit(solution)/shard_map/ppermute | solution.py:1172
  166.2 63.3 %collective-permute-start.1 = (bf16[256,768]{1,0:T(8,128)(2,1)}, bf16[256,768]{1,0:T(8,128)(2,1)}, u32[]{:S(2)}, u32[]{:S(2)}) collective-permute-start(bf16[256,768]{1,0:T(8,128)(2,1)} %get-tuple-element.65), channel_id=1, source_target_pairs={{0,1},{1,0},{2,5},{3,4},{4,3},{5,2},{6,7},{7,6},{8,9},{9,8},{10,13... | collective-permute-start | bytes 1179656 | tf_op jit(solution)/shard_map/ppermute | solution.py:1173
  166.3 64.3 %collective-permute-start.2 = (bf16[256,768]{1,0:T(8,128)(2,1)}, bf16[256,768]{1,0:T(8,128)(2,1)S(1)}, u32[]{:S(2)}, u32[]{:S(2)}) collective-permute-start(bf16[256,768]{1,0:T(8,128)(2,1)} %get-tuple-element.66), channel_id=1, source_target_pairs={{0,0},{1,1},{2,4},{3,5},{4,2},{5,3},{6,6},{7,7},{8,8},{9,9},{10,12... | collective-permute-start | bytes 1179656 | tf_op jit(solution)/shard_map/ppermute | solution.py:1174
  168.6 24.9 %copy-start.19 = (f32[1,384]{1,0:T(1,128)S(1)}, f32[1,384]{1,0:T(1,128)}, u32[]{:S(2)}) copy-start(f32[1,384]{1,0:T(1,128)} %get-tuple-element.92) | copy-start | bytes 4612
  168.6 25.8 %copy-start.15 = (f32[1,768]{1,0:T(1,128)S(1)}, f32[1,768]{1,0:T(1,128)}, u32[]{:S(2)}) copy-start(f32[1,768]{1,0:T(1,128)} %get-tuple-element.95) | copy-start | bytes 9220
  193.6 4.3 %copy-start = (bf16[768,768]{1,0:T(8,128)(2,1)S(1)}, bf16[768,768]{1,0:T(8,128)(2,1)}, u32[]{:S(2)}) copy-start(bf16[768,768]{1,0:T(8,128)(2,1)} %get-tuple-element.57.x) | copy-start | bytes 3538948
  198.1 6.0 %copy-start.27 = (bf16[768,1152]{1,0:T(8,128)(2,1)S(1)}, bf16[768,1152]{1,0:T(8,128)(2,1)}, u32[]{:S(2)}) copy-start(bf16[768,1152]{1,0:T(8,128)(2,1)} %get-tuple-element.88) | copy-start | bytes 5308420
  198.1 6.0 %copy-start.31 = (bf16[1024,384]{1,0:T(8,128)(2,1)S(1)}, bf16[1024,384]{1,0:T(8,128)(2,1)}, u32[]{:S(2)}) copy-start(bf16[1024,384]{1,0:T(8,128)(2,1)} %get-tuple-element.75) | copy-start | bytes 2359300
  198.2 6.0 %copy-start.33 = (bf16[1024,384]{1,0:T(8,128)(2,1)S(1)}, bf16[1024,384]{1,0:T(8,128)(2,1)}, u32[]{:S(2)}) copy-start(bf16[1024,384]{1,0:T(8,128)(2,1)} %get-tuple-element.82) | copy-start | bytes 2359300
  198.2 6.0 %copy-start.35 = (bf16[1024,384]{1,0:T(8,128)(2,1)S(1)}, bf16[1024,384]{1,0:T(8,128)(2,1)}, u32[]{:S(2)}) copy-start(bf16[1024,384]{1,0:T(8,128)(2,1)} %get-tuple-element.86) | copy-start | bytes 2359300
  198.2 6.0 %copy-start.37 = (bf16[512,384]{1,0:T(8,128)(2,1)S(1)}, bf16[512,384]{1,0:T(8,128)(2,1)}, u32[]{:S(2)}) copy-start(bf16[512,384]{1,0:T(8,128)(2,1)} %get-tuple-element.81) | copy-start | bytes 1179652
  223.5 9.7 %copy-start.34 = (bf16[1024,384]{1,0:T(8,128)(2,1)S(1)}, bf16[1024,384]{1,0:T(8,128)(2,1)}, u32[]{:S(2)}) copy-start(bf16[1024,384]{1,0:T(8,128)(2,1)} %get-tuple-element.82) | copy-start | bytes 2359300
  223.5 9.7 %copy-start.36 = (bf16[1024,384]{1,0:T(8,128)(2,1)S(1)}, bf16[1024,384]{1,0:T(8,128)(2,1)}, u32[]{:S(2)}) copy-start(bf16[1024,384]{1,0:T(8,128)(2,1)} %get-tuple-element.86) | copy-start | bytes 2359300
  223.5 9.7 %copy-start.38 = (bf16[512,384]{1,0:T(8,128)(2,1)S(1)}, bf16[512,384]{1,0:T(8,128)(2,1)}, u32[]{:S(2)}) copy-start(bf16[512,384]{1,0:T(8,128)(2,1)} %get-tuple-element.81) | copy-start | bytes 1179652
  223.6 8.1 %copy-start.1 = (f32[1024,768]{1,0:T(8,128)S(1)}, f32[1024,768]{1,0:T(8,128)}, u32[]{:S(2)}) copy-start(f32[1024,768]{1,0:T(8,128)} %slice.65) | copy-start | bytes 9437188
  223.6 14.9 %collective-permute-start.5 = (bf16[768,768]{1,0:T(8,128)(2,1)S(1)}, bf16[768,768]{1,0:T(8,128)(2,1)S(1)}, u32[]{:S(2)}, u32[]{:S(2)}) collective-permute-start(bf16[768,768]{1,0:T(8,128)(2,1)S(1)} %pad_maximum_fusion.1), channel_id=1, source_target_pairs={{0,4},{4,0},{1,5},{5,1},{2,6},{6,2},{3,7},{7,3},{8,12},{12,8},{9,1... | collective-permute-start | bytes 3538952 | tf_op jit(solution)/shard_map/ppermute | solution.py:33
  243.3 5.0 %copy-start.5 = (bf16[768,768]{1,0:T(8,128)(2,1)S(1)}, bf16[768,768]{1,0:T(8,128)(2,1)}, u32[]{:S(2)}) copy-start(bf16[768,768]{1,0:T(8,128)(2,1)} %copy-done.4) | copy-start | bytes 3538948
  243.3 5.0 %copy-start.6 = (f32[768,768]{1,0:T(8,128)S(1)}, f32[768,768]{1,0:T(8,128)}, u32[]{:S(2)}) copy-start(f32[768,768]{1,0:T(8,128)} %get-tuple-element.67) | copy-start | bytes 7077892
  341.5 3.5 collective-permute-start.6
  344.4 1.8 collective-permute-start.7
  (25 other events, 51.1 us)
Sparse Core Ops, SparseCore 0:
  145.9 62.0 reduce-scatter.1
  241.4 84.5 all-reduce.4
where the time goes:
time: 363 us; the launch traced here: 359 us
  Pallas kernels  263 us (72%)
  local copies, waits for them, and re-layouts  30 us (8%)
  other arithmetic  19.3 us (5%)
  matrix products  18.2 us (5%)
  between operations  15.2 us (4%)
  starting transfers between devices  12.1 us (3%)
    pallas_call x1, Pallas kernels, finish(): pl.pallas_call(finish_kernel, in_specs=[local_space, local_space], out_sp...  88.3 us
    pallas_call x1, Pallas kernels, forward_pass(): pl.pallas_call(functools.partial(forward_kernel, square, pics), in_specs=...  76.6 us
    pallas_call x1, Pallas kernels, dense(): pl.pallas_call(dense_kernel, in_specs=[near] * 7 + [anywhere, anywhere],...  56.3 us
    pallas_call x2, Pallas kernels, attend_back(): pl.pallas_call(functools.partial(attend_back_kernel, pics), grid=(pairs,)...  37.6 us
    dot_general x1, matrix products, nt(): lax.dot_general(a, b, (((1,), (1,)), ((), ())), preferred_element_type=F32)  13.6 us
    ppermute x5, starting transfers between devices, swap(): return lax.ppermute(array, name, [(i, i ^ bit) for i in range(count)])  8.68 us
  transfers between devices with their start and end apart: 10, of which 1 were waited for; matrix products, arithmetic and copies ran while one was open for 14% of the time, Pallas kernels for 36%

commit v1 on v0

--- a/solution.py
+++ b/solution.py
@@ -231,51 +231,6 @@
     kgg_ref[...] = gain_sum
 
 
-def attend_back(aug, k, v, out, do, raw, query_gain, key_gain, bounds, pics):
-    length, width = k.shape
-    queries = do.shape[0]
-    pairs = width // 128
-    column = pl.BlockSpec((length, 128), lambda p: (0, p))
-    own = pl.BlockSpec((queries, 128), lambda p: (0, p))
-    gain = pl.BlockSpec((1, 128), lambda p: (0, p))
-    return pl.pallas_call(
-        functools.partial(attend_back_kernel, pics),
-        grid=(pairs,),
-        in_specs=[
-            pl.BlockSpec((2, queries, 128), lambda p: (p, 0, 0)),
-            column,
-            column,
-            own,
-            own,
-            column,
-            pl.BlockSpec((length, 128), lambda p: (0, pairs + p)),
-            gain,
-            gain,
-            pl.BlockSpec((8, 128), lambda p: (0, 0)),
-        ],
-        out_specs=[own, column, column, gain, gain],
-        scratch_shapes=[
-            pltpu.VMEM((2, length, 128), BF16),
-            pltpu.VMEM((2, length, 128), BF16),
-            pltpu.VMEM((2, queries, 128), BF16),
-            pltpu.VMEM((2, queries, 128), F32),
-            pltpu.VMEM((length, 128), F32),
-        ],
-        out_shape=[
-            jax.ShapeDtypeStruct((queries, width), BF16),
-            jax.ShapeDtypeStruct((length, width), BF16),
-            jax.ShapeDtypeStruct((length, width), BF16),
-            jax.ShapeDtypeStruct((1, width), F32),
-            jax.ShapeDtypeStruct((1, width), F32),
-        ],
-        compiler_params=pltpu.CompilerParams(vmem_limit_bytes=VMEM_LIMIT),
-        cost_estimate=pl.CostEstimate(
-            flops=40 * length * queries * width, bytes_accessed=length * width * 20, transcendentals=0
-        ),
-        name="attend_back",
-    )(aug, k, v, out, do, raw, raw, query_gain, key_gain, bounds)
-
-
 def shared_keys_kernel(dk_ref, dv_ref, gotk_ref, gotv_ref, rawk_ref, kg_ref, outk_ref, outv_ref, kgg_ref):
     count = outk_ref.shape[0]
     part = count // 2
@@ -289,27 +244,6 @@
         gain_sum = gain_sum + more
         outv_ref[rows, :] = (own(dv_ref).astype(F32) + gotv_ref[rows, :].astype(F32)).astype(BF16)
     kgg_ref[...] = gain_sum
-
-
-def shared_keys(dk, dv, got_k, got_v, raw, key_gain):
-    length, width = dk.shape
-    pairs = width // 128
-    column = pl.BlockSpec((length, 128), lambda p: (0, p))
-    own = pl.BlockSpec((length // 2, 128), lambda p: (0, p))
-    gain = pl.BlockSpec((1, 128), lambda p: (0, p))
-    return pl.pallas_call(
-        shared_keys_kernel,
-        grid=(pairs,),
-        in_specs=[column, column, own, own, pl.BlockSpec((length, 128), lambda p: (0, pairs + p)), gain],
-        out_specs=[own, own, gain],
-        out_shape=[
-            jax.ShapeDtypeStruct((length // 2, width), BF16),
-            jax.ShapeDtypeStruct((length // 2, width), BF16),
-            jax.ShapeDtypeStruct((1, width), F32),
-        ],
-        compiler_params=pltpu.CompilerParams(vmem_limit_bytes=VMEM_LIMIT),
-        name="shared_keys",
-    )(dk, dv, got_k, got_v, raw, key_gain)
 
 
 def gelu_pair(h):
@@ -894,6 +828,8 @@
     cols_send.wait_recv()
     total = (forward[pl.ds(0, model), lanes(core)] + cols_in[...].astype(F32)).astype(BF16)
     eighth = model // 8
+    filled_rows = 2 * tile + eighth
+    packed[:, filled_rows:, :] = jnp.zeros((4, packed.shape[1] - filled_rows, model), BF16)
     for c in range(4):
         for h in range(2):
             at = (2 * c + h) * eighth
@@ -925,7 +861,7 @@
             jax.ShapeDtypeStruct((tokens, model), F32),
             jax.ShapeDtypeStruct((length, width), BF16),
             jax.ShapeDtypeStruct((length // 2, width), BF16),
-            jax.ShapeDtypeStruct((4, 2 * tile + model // 8, model), BF16),
+            jax.ShapeDtypeStruct((4, -(-(2 * tile + model // 8) // 64) * 64, model), BF16),
             jax.ShapeDtypeStruct((1, model), F32),
         ],
         scratch_shapes=[
@@ -958,17 +894,41 @@
     )(out, shared_out, x, grad, out_matrix, gain, bounds, up, down)
 
 
-def finish_kernel(
-    grad_ref, mix_ref, out_ref, total_ref, gains_ref,
-    relay, final, core_got, chunks, gain_parts, chunk_got, gain_got, sent, got, local_sem,
-):
+def add(*terms):
+    total = terms[0].astype(F32)
+    for term in terms[1:]:
+        total = total + term.astype(F32)
+    return total
+
+
+def backward_kernel(square, pics, *refs):
+    refs = list(refs)
+    take = lambda count: [refs.pop(0) for _ in range(count)]
+    names = ("aug", "k", "v", "out", "do", "raw", "normed")
+    row_in = dict(zip(names, take(7)))
+    shared_in = dict(zip(names, take(7)))
+    mix_in, x_in, midg_in, gain_first, gain_query, gain_key, gain_second_grad, bounds_ref = take(8)
+    if square:
+        packed_in, keep_in, cross_in, third_in = take(4)
+        output_ref, grad_out, total_ref, gains_ref, up_ref, down_ref, outw_ref = take(7)
+    else:
+        grad_own, mix_grad_ref, gains_sum = take(3)
+    names = names[:-1]
+    row = dict(zip(names, take(6)))
+    shared = dict(zip(names, take(6)))
+    normed, weight, x, midg = take(4)
+    kaug, vaug, doaug, qsum, ksum, mixed, part_k, part_v, got_k, got_v = take(10)
+    gain_sums, parts_out, parts_in = take(3)
+    if square:
+        grad_own, payload, gains_sum = take(3)
+        held, far_in, onward_out, onward_in, direct_in, line, near_in, second_sum, far_quarter, whole_line = take(10)
+        up_out, up_got, outw_out, outw_got = take(4)
+        relay, final, core_got, chunks, gain_parts, chunk_got, gain_got = take(7)
+    sent, got, load_sem, local_sem = take(4)
+
     chip, core, zp, zq = here()
     z = 2 * zp + zq
     sems = (sent, got)
-    part = out_ref.shape[1]
-    shard = mix_ref.shape[1] - 16
-    quarter = shard // 2
-    columns = mix_ref.shape[2]
     partner = (chip, 1 - core, zp, zq)
     keep = (chip, zp, core, zq)
     cross = (chip, zp, core, 1 - zq)
@@ -976,148 +936,381 @@
     near_x = (chip ^ 1, core, zp, zq)
     near_y = (chip ^ 2, core, zp, zq)
     along = [(chip, core, zp, 1 - zq), (chip, core, 1 - zp, zq), (chip, core, 1 - zp, 1 - zq)]
-    greet([partner, cross, near_x, near_y] + along, keep, moves)
-
-    mine, theirs = 2 * chip + core, 2 * chip + 1 - core
-    x_mine, x_other = 2 * (chip ^ 1) + core, 2 * (chip ^ 1) + 1 - core
-    y_mine, y_other = 2 * (chip ^ 2) + core, 2 * (chip ^ 2) + 1 - core
-    far_mine, far_other = 2 * (chip ^ 3) + core, 2 * (chip ^ 3) + 1 - core
-    first = remote(mix_ref.at[far_mine], relay.at[0], sems, 0, near_y)
-    second = remote(mix_ref.at[far_other], relay.at[1], sems, 1, near_x)
-    first.start()
-    second.start()
-    direct_x = remote(mix_ref.at[x_other], final.at[0], sems, 2, near_x)
-    direct_y = remote(mix_ref.at[y_mine], final.at[1], sems, 3, near_y)
-    direct_x.start()
-    direct_y.start()
-
-    own = pl.ds(pl.multiple_of(zq * part, 16), part)
-    own_row = remote(grad_ref.at[own], out_ref.at[zq], sems, 4, keep)
-    own_shared = remote(grad_ref.at[pl.ds(2 * part, part)], out_ref.at[2], sems, 5, keep)
-    stay_row = pltpu.make_async_copy(grad_ref.at[own], out_ref.at[zq], local_sem.at[0])
-    stay_shared = pltpu.make_async_copy(grad_ref.at[pl.ds(2 * part, part)], out_ref.at[2], local_sem.at[1])
-
-    @pl.when(moves)
-    def _():
-        own_row.start()
-        own_shared.start()
-
-    @pl.when(jnp.logical_not(moves))
-    def _():
-        stay_row.start()
-        stay_shared.start()
-
-    cross_row = remote(grad_ref.at[rows_at((1 - zq) * part, part)], out_ref.at[zq], sems, 6, cross)
-    cross_row.start()
-
-    def add(*terms):
-        total = terms[0].astype(F32)
-        for term in terms[1:]:
-            total = total + term.astype(F32)
-        return total
-
-    first.wait_recv()
-    relay[2] = add(relay[0], mix_ref[x_mine]).astype(BF16)
-    onward_x = remote(relay.at[2], final.at[2], sems, 7, near_x)
-    onward_x.start()
-    second.wait_recv()
-    relay[3] = add(relay[1], mix_ref[y_other]).astype(BF16)
-    onward_y = remote(relay.at[3], final.at[3], sems, 8, near_y)
-    onward_y.start()
-    direct_x.wait_recv()
-    onward_y.wait_recv()
-    relay[4] = add(mix_ref[theirs], final[0], final[3]).astype(BF16)
-    to_core = remote(relay.at[4], core_got, sems, 9, partner)
-    to_core.start()
-    direct_y.wait_recv()
-    onward_x.wait_recv()
-    kept = add(mix_ref[mine], final[1], final[2])
+    tokens, model = x.shape
+    part = tokens // 3
+    half, length = 2 * part, 4 * part
+    width = model // 2
+    queries = half
+    waits = []
+
+    def load(source, target, at):
+        copy = pltpu.make_async_copy(source, target, load_sem.at[at])
+        copy.start()
+        return copy
+
+    def send(source, target, at, device):
+        copy = remote(source, target, sems, at, device)
+        copy.start()
+        waits.append(copy)
+        return copy
+
+    if square:
+        rows_count = packed_in.shape[1]
+        span = rows_count // 2
+        first_half, second_half = pl.ds(0, span), pl.ds(span, span)
+        held_loads = [
+            load(packed_in.at[chip ^ 1, first_half], held.at[0], 24),
+            load(packed_in.at[chip ^ 2, second_half], held.at[1], 25),
+            load(packed_in.at[chip, first_half], held.at[2], 26),
+            load(packed_in.at[chip, second_half], held.at[3], 27),
+        ]
+    shared_loads = [load(shared_in[name], shared[name], i) for i, name in enumerate(names)]
+    row_loads = [load(row_in[name], row[name], 6 + i) for i, name in enumerate(names)]
+    late_loads = [
+        load(row_in["normed"], normed.at[pl.ds(0, length)], 12),
+        load(shared_in["normed"].at[rows_at(zq * part, part)], normed.at[pl.ds(length, part)], 13),
+        load(
+            shared_in["normed"].at[rows_at((2 + zq) * part, part)], normed.at[pl.ds(length + part, part)], 14
+        ),
+        load(mix_in, weight, 15),
+        load(x_in, x, 16),
+        load(midg_in, midg, 17),
+    ]
+    if square:
+        greet([partner, cross, near_x, near_y] + along, keep, moves)
+        bulk_first = send(packed_in.at[chip ^ 3, first_half], far_in.at[0], 0, near_y)
+        bulk_second = send(packed_in.at[chip ^ 3, second_half], far_in.at[1], 1, near_x)
+        bulk_x = send(packed_in.at[chip ^ 1, second_half], direct_in.at[0], 2, near_x)
+        bulk_y = send(packed_in.at[chip ^ 2, first_half], direct_in.at[1], 3, near_y)
+
+        def collect(sources, target, at, turn):
+            moved = [
+                remote(sources[0], target.at[zq], sems, at, keep),
+                remote(sources[2], target.at[2], sems, at + 1, keep),
+            ]
+            stays = [
+                pltpu.make_async_copy(sources[0], target.at[zq], local_sem.at[2 * turn]),
+                pltpu.make_async_copy(sources[2], target.at[2], local_sem.at[2 * turn + 1]),
+            ]
+            crossed = remote(sources[1], target.at[zq], sems, at + 2, cross)
+
+            @pl.when(moves)
+            def _():
+                for copy in moved:
+                    copy.start()
+
+            @pl.when(jnp.logical_not(moves))
+            def _():
+                for copy in stays:
+                    copy.start()
+
+            crossed.start()
+            return moved, stays, crossed
+
+        def collected(copies):
+            moved, stays, crossed = copies
+            crossed.wait()
+
+            @pl.when(moves)
+            def _():
+                for copy in moved:
+                    copy.wait()
+
+            @pl.when(jnp.logical_not(moves))
+            def _():
+                for copy in stays:
+                    copy.wait()
+
+        output_copies = collect((keep_in, cross_in, third_in), output_ref, 4, 0)
+    else:
+        greet([partner, along[0]])
+
+    gain_sums[...] = jnp.zeros_like(gain_sums)
+
+    def attend_back(bufs, bounds, count, q_lanes_to, k_to, v_to, at):
+        def one(p, _):
+            lanes = pl.ds(pl.multiple_of(p * 128, 128), 128)
+            key_lanes = pl.ds(pl.multiple_of(width + p * 128, 128), 128)
+            attend_back_kernel(
+                pics, bufs["aug"].at[pl.ds(2 * p, 2)], bufs["k"].at[:, lanes], bufs["v"].at[:, lanes],
+                bufs["out"].at[:, lanes], bufs["do"].at[:, lanes], bufs["raw"].at[:, lanes],
+                bufs["raw"].at[:, key_lanes], gain_query.at[:, lanes], gain_key.at[:, lanes], bounds,
+                q_lanes_to(p), k_to(p), v_to(p), gain_sums.at[pl.ds(at, 1), lanes], gain_sums.at[pl.ds(at + 1, 1), lanes],
+                kaug, vaug, doaug.at[:, pl.ds(0, count)], qsum.at[:, pl.ds(0, count)], ksum,
+            )
+            return 0
+
+        lax.fori_loop(0, width // 128, one, 0)
+
+    def mixed_at(start, count, side):
+        return lambda p: mixed.at[pl.ds(start, count), pl.ds(pl.multiple_of(side * width + p * 128, 128), 128)]
+
+    whole_lanes = lambda ref: lambda p: ref.at[:, pl.ds(pl.multiple_of(p * 128, 128), 128)]
+    for copy in shared_loads:
+        copy.wait()
+    attend_back(
+        shared, bounds_ref.at[1], queries, mixed_at(length, queries, 0), whole_lanes(part_k), whole_lanes(part_v), 0
+    )
+    side_sends = []
     for i in range(2):
-        chunks[2 * core + i] = kept[i * quarter : (i + 1) * quarter].astype(BF16)
-    to_core.wait_recv()
-    for i in range(2):
-        chunks[2 * (1 - core) + i] = core_got[i * quarter : (i + 1) * quarter]
-    gain_parts[0] = (kept[shard:] + core_got[shard:].astype(F32)).astype(BF16)
-    hops = [z ^ 1, z ^ 2, z ^ 3]
-    copies = []
-    for i in range(3):
-        copies.append(remote(chunks.at[hops[i]], chunk_got.at[i], sems, 10 + i, along[i]))
-        copies.append(remote(gain_parts.at[0], gain_got.at[i], sems, 13 + i, along[i]))
-    for copy in copies:
-        copy.start()
-    for copy in copies:
+        theirs = rows_at((2 * i + 1 - zq) * part, part)
+        there = pl.ds(i * part, part)
+        side_sends.append(send(part_k.at[theirs], got_k.at[there], 7 + 2 * i, along[0]))
+        side_sends.append(send(part_v.at[theirs], got_v.at[there], 8 + 2 * i, along[0]))
+    if square:
+        for copy in held_loads:
+            copy.wait()
+        bulk_first.wait_recv()
+        onward_out[0] = add(far_in[0], held[0]).astype(BF16)
+        bulk_on_x = send(onward_out.at[0], onward_in.at[0], 11, near_x)
+        bulk_second.wait_recv()
+        onward_out[1] = add(far_in[1], held[1]).astype(BF16)
+        bulk_on_y = send(onward_out.at[1], onward_in.at[1], 12, near_y)
+    for copy in row_loads:
+        copy.wait()
+    attend_back(
+        row, bounds_ref.at[0], length, mixed_at(0, length, 0), mixed_at(0, length, 1), mixed_at(0, length, 2), 2
+    )
+
+    for copy in side_sends:
         copy.wait_recv()
-    gains_ref[...] = add(gain_parts[0], gain_got[0], gain_got[1], gain_got[2])
-    chunk_got[3] = add(chunks[z], chunk_got[0], chunk_got[1], chunk_got[2]).astype(BF16)
-    spread = [remote(chunk_got.at[3], chunk_got.at[4 + i], sems, 16 + i, along[i]) for i in range(3)]
-    for copy in spread:
-        copy.start()
-
-    def place(index, values):
-        half, up = index // 2, index % 2
-        third = columns // 3
-        values = values.astype(F32)
-        for h in range(2):
-            for u in range(2):
-
-                @pl.when((half == h) & (up == u))
-                def _():
-                    for p in range(3):
-                        total_ref[u * quarter : (u + 1) * quarter, (2 * p + h) * third : (2 * p + h + 1) * third] = (
-                            values[:, p * third : (p + 1) * third]
-                        )
-
-    place(z, chunk_got[3])
-    for i in range(3):
-        spread[i].wait_recv()
-        place(hops[i], chunk_got[4 + i])
-    for copy in copies + spread + [first, second, direct_x, direct_y, onward_x, onward_y, to_core]:
+
+    def shared_pair(p, _):
+        lanes = pl.ds(pl.multiple_of(p * 128, 128), 128)
+        key_lanes = pl.ds(pl.multiple_of(width + p * 128, 128), 128)
+        shared_keys_kernel(
+            part_k.at[:, lanes], part_v.at[:, lanes], got_k.at[:, lanes], got_v.at[:, lanes],
+            shared["raw"].at[:, key_lanes], gain_key.at[:, lanes], mixed_at(length, queries, 1)(p),
+            mixed_at(length, queries, 2)(p), gain_sums.at[pl.ds(4, 1), lanes],
+        )
+        return 0
+
+    lax.fori_loop(0, width // 128, shared_pair, 0)
+    for copy in late_loads:
+        copy.wait()
+    other = 1 - core
+    block_rows = lambda side, b: (
+        rows_at(side * half + b * part, part) if b < 2 else rows_at(length + side * part, part)
+    )
+    for b in range(3):
+        parts_out[pl.ds(b * part, part), :] = nt(mixed[block_rows(other, b), :], weight[...]).astype(BF16)
+    part_send = send(parts_out, parts_in, 13, partner)
+    if square:
+        bulk_y.wait_recv()
+        bulk_on_x.wait_recv()
+        bulk_x.wait_recv()
+        bulk_on_y.wait_recv()
+        quarter_rows = rows_count // 4
+        first_sum = add(held[2], onward_in[0], direct_in[1]).astype(BF16)
+        second_half_sum = add(held[3], onward_in[1], direct_in[0]).astype(BF16)
+        for i in range(2):
+            line[i] = first_sum[i * quarter_rows : (i + 1) * quarter_rows]
+            line[2 + i] = second_half_sum[i * quarter_rows : (i + 1) * quarter_rows]
+        line_near = [send(line.at[2 * i + 1 - zq], near_in.at[i], 14 + i, along[0]) for i in range(2)]
+    shard = model // 8
+    if square:
+        for i in range(3):
+            lanes = slice(i * width, (i + 1) * width)
+            value = tn(normed[...], mixed[:, lanes]).astype(BF16)
+            for p in range(8):
+                payload[p, :shard, lanes] = value[p * shard : (p + 1) * shard]
+    else:
+        for i in range(3):
+            lanes = slice(i * width, (i + 1) * width)
+            mix_grad_ref[:, lanes] = tn(normed[...], mixed[:, lanes]).astype(BF16)
+    part_send.wait_recv()
+    first_sum_gain = jnp.zeros((1, model), F32)
+    for b in range(3):
+        rows = pl.ds(b * part, part)
+        upstream = nt(mixed[block_rows(core, b), :], weight[...]) + parts_in[rows, :].astype(F32)
+        n, r = norm_parts(x[rows, :].astype(F32))
+        value, more = norm_back(upstream, n, r, gain_first[...])
+        first_sum_gain = first_sum_gain + more
+        grad_own[rows, :] = (midg[rows, :] + value).astype(BF16)
+    gains_sum[...] = jnp.zeros_like(gains_sum)
+    gains_sum[0:1, :] = first_sum_gain
+    mine_lanes = pl.ds(pl.multiple_of(core * width, 128), width)
+    gains_sum[1:2, mine_lanes] = gain_sums[0:1, :] + gain_sums[2:3, :]
+    gains_sum[2:3, mine_lanes] = gain_sums[3:4, :] + gain_sums[4:5, :]
+    gains_sum[3:4, :] = gain_second_grad[...]
+
+    if square:
+        grad_copies = collect(
+            (
+                grad_own.at[rows_at(zq * part, part)],
+                grad_own.at[rows_at((1 - zq) * part, part)],
+                grad_own.at[pl.ds(half, part)],
+            ),
+            grad_out, 16, 1,
+        )
+        for p in range(8):
+            payload[p, shard:, :] = jnp.zeros((16, 3 * width), BF16)
+            payload[p, shard:, :shard] = gains_sum[:, p * shard : (p + 1) * shard].astype(BF16)
+        mine, theirs = 2 * chip + core, 2 * chip + 1 - core
+        x_mine, x_other = 2 * (chip ^ 1) + core, 2 * (chip ^ 1) + 1 - core
+        y_mine, y_other = 2 * (chip ^ 2) + core, 2 * (chip ^ 2) + 1 - core
+        far_mine, far_other = 2 * (chip ^ 3) + core, 2 * (chip ^ 3) + 1 - core
+        first = send(payload.at[far_mine], relay.at[0], 19, near_y)
+        second = send(payload.at[far_other], relay.at[1], 20, near_x)
+        direct_x = send(payload.at[x_other], final.at[0], 21, near_x)
+        direct_y = send(payload.at[y_mine], final.at[1], 22, near_y)
+
+        for copy in line_near:
+            copy.wait_recv()
+        for i in range(2):
+            second_sum[i] = add(line[2 * i + zq], near_in[i]).astype(BF16)
+        line_far = send(second_sum.at[1 - zp], far_quarter, 23, along[1])
+        first.wait_recv()
+        relay[2] = add(relay[0], payload[x_mine]).astype(BF16)
+        onward_x = send(relay.at[2], final.at[2], 24, near_x)
+        second.wait_recv()
+        relay[3] = add(relay[1], payload[y_other]).astype(BF16)
+        onward_y = send(relay.at[3], final.at[3], 25, near_y)
+        direct_x.wait_recv()
+        onward_y.wait_recv()
+        relay[4] = add(payload[theirs], final[0], final[3]).astype(BF16)
+        to_core = send(relay.at[4], core_got, 26, partner)
+        direct_y.wait_recv()
+        onward_x.wait_recv()
+        kept = add(payload[mine], final[1], final[2])
+        quarter = shard // 2
+        for i in range(2):
+            chunks[2 * core + i] = kept[i * quarter : (i + 1) * quarter].astype(BF16)
+        to_core.wait_recv()
+        for i in range(2):
+            chunks[2 * (1 - core) + i] = core_got[i * quarter : (i + 1) * quarter]
+        gain_parts[0] = (kept[shard:] + core_got[shard:].astype(F32)).astype(BF16)
+        hops = [z ^ 1, z ^ 2, z ^ 3]
+        copies = []
+        for i in range(3):
+            copies.append(send(chunks.at[hops[i]], chunk_got.at[i], 27 + i, along[i]))
+            copies.append(send(gain_parts.at[0], gain_got.at[i], 30 + i, along[i]))
+        line_far.wait_recv()
+        whole_line[z] = add(second_sum[zp], far_quarter[...]).astype(BF16)
+        line_back = send(whole_line.at[z], whole_line.at[z], 33, along[1])
+        for copy in copies:
+            copy.wait_recv()
+        gains_ref[...] = add(gain_parts[0], gain_got[0], gain_got[1], gain_got[2])
+        chunk_got[3] = add(chunks[z], chunk_got[0], chunk_got[1], chunk_got[2]).astype(BF16)
+        spread = [send(chunk_got.at[3], chunk_got.at[4 + i], 34 + i, along[i]) for i in range(3)]
+        line_back.wait_recv()
+        line_last = [
+            send(whole_line.at[z], whole_line.at[z], 37, along[0]),
+            send(whole_line.at[z ^ 2], whole_line.at[z ^ 2], 38, along[0]),
+        ]
+
+        def place(index, values):
+            side, up = index // 2, index % 2
+            values = values.astype(F32)
+            rows = rows_at(up * quarter, quarter)
+            for p in range(3):
+                lanes = pl.ds(pl.multiple_of((2 * p + side) * width, 128), width)
+                total_ref[rows, lanes] = values[:, p * width : (p + 1) * width]
+
+        place(z, chunk_got[3])
+        for i in range(3):
+            spread[i].wait_recv()
+            place(hops[i], chunk_got[4 + i])
+
+        for copy in line_last:
+            copy.wait_recv()
+        flat = jnp.concatenate([whole_line[i] for i in range(4)], axis=0)
+        tile = down_ref.shape[0]
+        down_ref[...] = flat[:tile].astype(F32)
+        ups = [flat[tile + 2 * shard * i : tile + 2 * shard * (i + 1)] for i in range(2)]
+        outs = flat[2 * tile : 2 * tile + shard]
+        for i in range(2):
+            up_out[i] = jnp.where(core == 0, ups[i][shard:], ups[i][:shard])
+        outw_out[...] = jnp.where(core == 0, outs[:, width:], outs[:, :width])
+        up_send = send(up_out, up_got, 39, partner)
+        outw_send = send(outw_out, outw_got, 40, partner)
+
+        def place_up(side, i, values):
+            values = values.astype(F32)
+            for j in range(2):
+                lanes = pl.ds(pl.multiple_of((2 * (2 * i + j) + side) * tile, 128), tile)
+                up_ref[:, lanes] = values[:, j * tile : (j + 1) * tile]
+
+        for i in range(2):
+            place_up(core, i, jnp.where(core == 0, ups[i][:shard], ups[i][shard:]))
+        outw_ref[:, mine_lanes] = jnp.where(core == 0, outs[:, :width], outs[:, width:]).astype(F32)
+        up_send.wait_recv()
+        outw_send.wait_recv()
+        for i in range(2):
+            place_up(other, i, up_got[i])
+        outw_ref[:, pl.ds(pl.multiple_of(other * width, 128), width)] = outw_got[...].astype(F32)
+        collected(output_copies)
+        collected(grad_copies)
+    for copy in waits:
         copy.wait_send()
-    cross_row.wait()
-
-    @pl.when(moves)
-    def _():
-        own_row.wait()
-        own_shared.wait()
-
-    @pl.when(jnp.logical_not(moves))
-    def _():
-        stay_row.wait()
-        stay_shared.wait()
-
-
-def finish(grad, mix):
-    tokens, model = grad.shape
-    _, rows, columns = mix.shape
-    shard = rows - 16
-    local_space = pl.BlockSpec(memory_space=pltpu.VMEM)
-    buffers = lambda count, size: pltpu.VMEM((count, size, columns), BF16)
+
+
+def backward_pass(square, pics, row, shared, weights, gains, bounds, *more):
+    length, width = row[1].shape
+    model = 2 * width
+    part = length // 4
+    half, tokens = 2 * part, 3 * part
+    shard = model // 8
+    near = pl.BlockSpec(memory_space=pltpu.VMEM)
+    anywhere = pl.BlockSpec(memory_space=pl.ANY)
+    low = lambda *shape: (shape, BF16)
+    wide = lambda *shape: (shape, F32)
+    if square:
+        rows = more[0].shape[1]
+        tile = more[4]
+        more = more[:4]
+        outs = [
+            (low(3, part, model), anywhere),
+            (low(3, part, model), anywhere),
+            (wide(shard, 6 * width), near),
+            (wide(16, 3 * width), near),
+            (wide(shard, 8 * tile), near),
+            (wide(tile, model), near),
+            (wide(shard, model), near),
+        ]
+    else:
+        outs = [(low(tokens, model), near), (low(model, 3 * width), near), (wide(16, model), near)]
+    scratch = []
+    for queries in (length, half):
+        scratch += [
+            low(2 * (width // 128), queries, 128), low(length, width), low(length, width), low(queries, width),
+            low(queries, width), low(length, 2 * width),
+        ]
+    scratch += [
+        low(length + half, model), low(model, 3 * width), low(tokens, model), wide(tokens, model),
+        low(2, length, 128), low(2, length, 128), low(2, length, 128), wide(2, length, 128), wide(length, 128),
+        low(length + half, 3 * width), low(length, width), low(length, width), low(half, width), low(half, width),
+        wide(8, width), low(tokens, model), low(tokens, model),
+    ]
+    if square:
+        span = rows // 2
+        pieces = shard + 16
+        scratch += [
+            low(tokens, model), low(8, pieces, 3 * width), wide(16, model),
+            low(4, span, model), low(2, span, model), low(2, span, model), low(2, span, model), low(2, span, model),
+            low(4, rows // 4, model), low(2, rows // 4, model), low(2, rows // 4, model), low(rows // 4, model),
+            low(4, rows // 4, model),
+            low(2, shard, model), low(2, shard, model), low(shard, width), low(shard, width),
+            low(5, pieces, 3 * width), low(4, pieces, 3 * width), low(pieces, 3 * width), low(4, shard // 2, 3 * width),
+            low(1, 16, 3 * width), low(7, shard // 2, 3 * width), low(3, 16, 3 * width),
+        ]
     return pl.pallas_call(
-        finish_kernel,
-        in_specs=[local_space, local_space],
-        out_specs=[local_space, local_space, local_space],
-        out_shape=[
-            jax.ShapeDtypeStruct((3, tokens // 3, model), BF16),
-            jax.ShapeDtypeStruct((shard, 2 * columns), F32),
-            jax.ShapeDtypeStruct((16, columns), F32),
-        ],
-        scratch_shapes=[
-            buffers(5, rows),
-            buffers(4, rows),
-            pltpu.VMEM((rows, columns), BF16),
-            buffers(4, shard // 2),
-            buffers(1, 16),
-            buffers(7, shard // 2),
-            buffers(3, 16),
-            pltpu.SemaphoreType.DMA((19,)),
-            pltpu.SemaphoreType.DMA((19,)),
-            pltpu.SemaphoreType.DMA((2,)),
+        functools.partial(backward_kernel, square, pics),
+        in_specs=[anywhere] * 17 + [near] * 5 + [anywhere] * len(more),
+        out_specs=[spec for _, spec in outs],
+        out_shape=[jax.ShapeDtypeStruct(*shape) for shape, _ in outs],
+        scratch_shapes=[pltpu.VMEM(*shape) for shape in scratch]
+        + [
+            pltpu.SemaphoreType.DMA((41,)),
+            pltpu.SemaphoreType.DMA((41,)),
+            pltpu.SemaphoreType.DMA((28,)),
+            pltpu.SemaphoreType.DMA((4,)),
         ],
         compiler_params=pltpu.CompilerParams(
-            collective_id=3, has_side_effects=True, vmem_limit_bytes=VMEM_LIMIT
+            collective_id=2, has_side_effects=True, vmem_limit_bytes=62 * 1024 * 1024
         ),
-        name="finish",
-    )(grad, mix)
+        name="backward_pass",
+    )(*row, *shared, *weights, *gains, bounds, *more)
 
 
 def local(
@@ -1177,90 +1370,42 @@
     out_keep, out_cross, out_third, middle_grad, grad, shared_grad, packed, second_gain_grad = dense(
         out, shared_out, own_tokens, grad_tokens, out_matrix, gain_second, bounds, up_half, down_half
     )
-    output = collect(out_keep, out_cross, out_third)
-
-    def reduce(grad):
-        return lax.psum(lax.psum_scatter(grad, rows, scatter_dimension=0, tiled=True), SEQ).astype(F32)
-
-    eighth = model // 8
-    if square:
-        size = packed.shape[1]
-        mine = lax.psum_scatter(packed.reshape(4 * size, model), "chip", scatter_dimension=0, tiled=True)
-        mine = lax.psum(mine, SEQ)
-        down_out = mine[:tile].astype(F32)
-        up_mine = mine[tile : 2 * tile].reshape(2, 2, shard, 2, tile).transpose(1, 2, 0, 3, 4)
-        up_mine = up_mine.reshape(2, shard, 4, tile)
-        outw_mine = mine[2 * tile :].reshape(shard, 2, width).transpose(1, 0, 2)
-        up_other = swap(pick(up_mine, 1 - core).reshape(shard, 4 * tile), "core").reshape(shard, 4, tile)
-        outw_other = swap(pick(outw_mine, 1 - core), "core")
-        up_mine, outw_mine = pick(up_mine, core), pick(outw_mine, core)
-        low = jnp.where(core == 0, up_mine, up_other)
-        high = jnp.where(core == 0, up_other, up_mine)
-        up_out = jnp.stack([low, high], axis=2).reshape(shard, hidden).astype(F32)
-        low = jnp.where(core == 0, outw_mine, outw_other)
-        high = jnp.where(core == 0, outw_other, outw_mine)
-        outw_out = jnp.concatenate([low, high], axis=1).astype(F32)
+    row_side = (aug, k, v, out, grad, raw, normed)
+    shared_side = (shared_aug, shared_k, shared_v, shared_out, shared_grad, shared_raw, shared_normed)
+    weights = (mix_half, own_tokens, middle_grad)
+    gains = (gain_first, gain_query, gain_key, second_gain_grad)
+    if square:
+        output, input_out, mix_out, gains_out, up_out, down_out, outw_out = backward_pass(
+            True, pics, row_side, shared_side, weights, gains, bounds, packed, out_keep, out_cross, out_third, tile
+        )
+        gains_out = gains_out[:4, :shard]
     else:
+        input_grad, mix_grad, gain_grads = backward_pass(
+            False, pics, row_side, shared_side, weights, gains, bounds
+        )
+
+        def reduce(grad):
+            return lax.psum(lax.psum_scatter(grad, rows, scatter_dimension=0, tiled=True), SEQ).astype(F32)
+
+        output = collect(out_keep, out_cross, out_third)
+        first, second = input_grad[:part], input_grad[part:half]
+        input_out = collect(
+            jnp.where(zq == 0, first, second), jnp.where(zq == 0, second, first), input_grad[half:]
+        )
         own_core = jnp.arange(2) == core
+        eighth = model // 8
         down_grad = packed[:, None, :tile]
         down_out = reduce(jnp.where(own_core[None, :, None, None], down_grad, 0).reshape(hidden, model))
         up_grad = packed[:, tile : 2 * tile].reshape(4, 2, 2 * eighth, 2, tile).transpose(0, 2, 1, 3, 4)
         up_grad = up_grad.reshape(model, 4, 1, tile)
         up_out = reduce(jnp.where(own_core[None, None, :, None], up_grad, 0).reshape(model, hidden))
-        out_grad = packed[:, 2 * tile :].reshape(4, eighth, 2, width).transpose(0, 2, 1, 3)
+        out_grad = packed[:, 2 * tile : 2 * tile + eighth].reshape(4, eighth, 2, width).transpose(0, 2, 1, 3)
         out_grad = out_grad.reshape(model, 1, width)
         outw_out = reduce(jnp.where(own_core[None, :, None], out_grad, 0).reshape(model, model))
-
-    shared_dq, part_k, part_v, shared_qgg, _ = attend_back(
-        shared_aug, shared_k, shared_v, shared_out, shared_grad, shared_raw, gain_query, gain_key,
-        bounds[1], pics,
-    )
-
-    def to_side(array):
-        return swap(pick(array.reshape(2, 2, part, width), 1 - zq, 1), "zq").reshape(half, width)
-
-    got_k, got_v = to_side(part_k), to_side(part_v)
-    dq, dk, dv, qgg, kgg = attend_back(
-        aug, k, v, out, grad, raw, gain_query, gain_key, bounds[0], pics
-    )
-    shared_dk, shared_dv, shared_kgg = shared_keys(part_k, part_v, got_k, got_v, shared_raw, gain_key)
-    mixed = jnp.concatenate(
-        [jnp.concatenate([dq, shared_dq]), jnp.concatenate([dk, shared_dk]), jnp.concatenate([dv, shared_dv])],
-        axis=1,
-    )
-    own_shared = pick(shared_normed.reshape(2, 2, part, model), zq, 1).reshape(half, model)
-    mix_grad = tn(jnp.concatenate([normed, own_shared]), mixed).astype(BF16)
-    partial = nt(mixed, mix_half)
-    row_partial = partial[:length].reshape(2, half, model)
-    shared_partial = partial[length:].reshape(2, part, model)
-    mine = jnp.concatenate([pick(row_partial, core), pick(shared_partial, core)])
-    sent = jnp.concatenate([pick(row_partial, 1 - core), pick(shared_partial, 1 - core)])
-    normed_grad = mine + swap(sent.astype(BF16), "core").astype(F32)
-    n_first, r_first = norm_parts(own_tokens.astype(F32))
-    input_part, first_gain_grad = norm_back(normed_grad, n_first, r_first, gain_first)
-    input_grad = (middle_grad + input_part).astype(BF16)
-
-    def place_heads(values):
-        return jnp.where(jnp.arange(2)[:, None] == core, values, 0.0).reshape(1, model)
-
-    gain_grads = jnp.concatenate(
-        [first_gain_grad, place_heads(qgg + shared_qgg), place_heads(kgg + shared_kgg), second_gain_grad]
-    )
-    gain_grads = gain_grads.reshape(4, 2 * chips, shard).transpose(1, 0, 2).astype(BF16)
-    if square:
-        gain_rows = jnp.pad(gain_grads, ((0, 0), (0, 12), (0, 3 * width - shard)))
-        payload = jnp.concatenate([mix_grad.reshape(2 * chips, shard, 3 * width), gain_rows], axis=1)
-        input_out, mix_out, gains_out = finish(input_grad, payload)
-        gains_out = gains_out[:4, :shard]
-    else:
-        first, second = input_grad[:part], input_grad[part:half]
-        input_out = collect(
-            jnp.where(zq == 0, first, second), jnp.where(zq == 0, second, first), input_grad[half:]
+        mix_out = reduce(
+            jnp.where(own_core[None, None, :, None], mix_grad.reshape(model, 3, 1, width), 0).reshape(model, 6 * width)
         )
-        spread_mix = jnp.where(
-            jnp.arange(2)[None, None, :, None] == core, mix_grad.reshape(model, 3, 1, width), 0
-        ).reshape(model, 6 * width)
-        mix_out = reduce(spread_mix)
+        gain_grads = gain_grads[:4].reshape(4, 2 * chips, shard).transpose(1, 0, 2).astype(BF16)
         gains_out = reduce(gain_grads).reshape(4, shard)
     return (
         output, input_out, gains_out[0], mix_out, gains_out[1], gains_out[2], outw_out, gains_out[3],

time: 363 us -> 309 us (0.85)
  Pallas kernels: 263 us -> 285 us
  matrix products: 18.2 us -> 0 us
  other arithmetic: 19.3 us -> 1.89 us
  between operations: 15.2 us -> 1.15 us
  local copies, waits for them, and re-layouts: 30 us -> 16.7 us
  starting transfers between devices: 12.1 us -> 0 us
    pallas_call x4 -> x1, Pallas kernels: 130 us -> 153 us  [backward_pass(): pl.pallas_call(functools.partial(backward_kernel, square, pics), in_specs...]
    dot_general x2 -> x0, matrix products: 18.2 us -> none  [the longest x1 13.6 us: nt(): lax.dot_general(a, b, (((1,), (1,)), ((), ())), preferred_element_type=F32)]
    ppermute x8 -> x0, starting transfers between devices: 12 us -> none  [the longest x5 8.68 us: swap(): return lax.ppermute(array, name, [(i, i ^ bit) for i in range(count)])]
    convert_element_type x5 -> x0, other arithmetic: 6.26 us -> none  [the longest x1 2.37 us: local(): down_out = mine[:tile].astype(F32)]
    squeeze x8 -> x1, local copies, waits for them, and re-layouts: 4.99 us -> 1.27 us  [local(): gain_query, gain_key = (query_first[0], key_first[0])]
    unnamed x82 -> x18, local copies, waits for them, and re-layouts: 5.79 us -> 8.61 us
  transfers between devices with their start and end apart: 10 -> 0, of which waited for: 1 -> 0; matrix products, arithmetic and copies ran while one was open for 14% -> 0% of each run, Pallas kernels for 36% -> 0%
where the time goes in v1:
time: 309 us; the launch traced here: 305 us
  Pallas kernels  285 us (92%)
  local copies, waits for them, and re-layouts  16.7 us (5%)
    pallas_call x1, Pallas kernels, backward_pass(): pl.pallas_call(functools.partial(backward_kernel, square, pics), in_specs...  153 us
    pallas_call x1, Pallas kernels, forward_pass(): pl.pallas_call(functools.partial(forward_kernel, square, pics), in_specs=...  76.6 us
    pallas_call x1, Pallas kernels, dense(): pl.pallas_call(dense_kernel, in_specs=[near] * 7 + [anywhere, anywhere],...  55.8 us
    unnamed x18, local copies, waits for them, and re-layouts  8.61 us

profile of v1, /device:TPU:0, one launch (start us, length us, event | category | flops | bytes accessed | tf_op | source)
XLA Modules:
  0.0 304.9 jit_solution(7635676605309620935)
XLA Ops:
  0.6 1.3 pad.8.refs_2_
  1.9 1.3 fusion.8.refs_4_
  3.2 1.1 reshape.32
  4.3 0.0 copy-start.4
  4.4 0.2 copy.28
  4.6 1.1 reshape.33.refs_3_
  5.7 0.4 reshape.34
  6.2 0.2 copy.27
  6.4 1.0 reshape.35.refs_5_
  7.4 76.6 %forward_pass.1 = (bf16[768,768]{1,0:T(8,128)(2,1)}, s32[2,8,128]{2,1,0:T(8,128)}, bf16[768,1152]{1,0:T(8,128)(2,1)}, f32[1,768]{1,0:T(1,128)}, f32[2,1,384]{2,1...) custom-call(bf16[3,256,768]{2,1,0:T(8,128)(2,1)} %refs_0_.1, ...), custom_call_target="tpu_custom_call" | custom-call | tf_op jit(solution)/shard_map/forward_pass/pallas_call | solution.py:668
  84.1 1.3 slice_bitcast_fusion
  85.4 0.6 pad_maximum_fusion.refs_17_
  85.9 55.8 %dense.1 = (bf16[256,768]{1,0:T(8,128)(2,1)}, bf16[256,768]{1,0:T(8,128)(2,1)}, bf16[256,768]{1,0:T(8,128)(2,1)}, f32[768,768]{1,0:T(8,128)}, bf16[1024,384]{1,0...) custom-call(bf16[1024,384]{1,0:T(8,128)(2,1)} %get-tuple-element.50.out_ref.refs_3_, ...), custom_call_target="tpu_custom_call" | custom-call | flops 28991029248 | bytes 18874368 | tf_op jit(solution)/shard_map/dense/pallas_call | solution.py:853
  141.7 152.8 %backward_pass.1 = (bf16[3,256,768]{2,1,0:T(8,128)(2,1)}, bf16[3,256,768]{2,1,0:T(8,128)(2,1)}, f32[96,2304]{1,0:T(8,128)}, f32[16,1152]{1,0:T(8,128)}, f32[96,3...) custom-call(bf16[6,1024,128]{2,1,0:T(8,128)(2,1)} %get-tuple-element.47.refs_0_, ...), custom_call_target="tpu_custom_call" | custom-call | tf_op jit(solution)/shard_map/backward_pass/pallas_call | solution.py:1297
  294.5 1.4 slice_bitcast_fusion.4
  295.9 2.5 copy.35
  298.3 1.0 copy.36
  299.3 0.6 copy-done.3
  299.9 0.9 copy.37
  300.8 0.2 copy-done.5
  301.0 0.7 copy.38
  301.8 1.0 copy.39
  302.8 0.7 copy-done
  303.5 1.0 copy.40
  (8 shorter events, 0.0 us)
Async XLA Ops:
  4.3 1.4 copy-start.4
  295.9 2.5 copy-start.2
  298.3 1.6 copy-start.3
  299.9 1.1 copy-start.5
  299.9 1.8 copy-start.1
  301.8 1.7 copy-start
